TPU v7x, 32 devices: a whole 2x2x4 slice. The times are simulated.
32 devices in a mesh: dp: 4 (over x, core), seq: 4 (over z), mp: 2 (over y).
Axes of the slice: x: 2, y: 2, z: 4, core: 2. Of those that a mesh axis runs over, the one named last changes fastest.
Arguments:
- queries: bfloat16 [4, 512, 2048], P('dp', 'seq', 'mp'), may hold values from -6 to 6
- keys: bfloat16 [4, 512, 2048], P('dp', 'seq', 'mp'), may hold values from -6 to 6
- values: bfloat16 [4, 512, 2048], P('dp', 'seq', 'mp'), may hold values from -6 to 6
- cross_queries: bfloat16 [4, 512, 2048], P('dp', 'seq', 'mp'), may hold values from -6 to 6
- neighbour_ids: int32 [4, 8, 2, 2], P('dp', 'seq'), may hold values from 0 to 5, as said below
- database: bfloat16 [4, 2, 6, 128, 2048], P('dp', None, None, None, 'mp'), may hold values from -6 to 6
- out_weight: bfloat16 [2048, 4096], P('mp'), may hold values from -2.5 to 2.5
Outputs:
- mixed: bfloat16 [4, 512, 4096], P('dp', 'seq', 'mp')
Inputs may be any that keep to these rules, and one draw needn't show every extreme that they name: `neighbour_ids`: entry [b, c, n, 0] is the database shard and [b, c, n, 1] the block of the n-th neighbour of span c of sequence b. Among the neighbours of the 2 spans held by one index of dp and seq, at most 3 name one shard; in every draw, for some seq index, the spans of every dp index name exactly 3 neighbours of one common shard.
All inputs are finite; a program needn't handle non-finite values.
Results may differ from a plain program's by a relative error of at most 0.012.
Values may be sent and summed in bfloat16 or wider, within the bound.
A program may use at most 128 MiB of HBM per device.

v0:
```python
import math

import jax
import jax.numpy as jnp
from jax import lax
from jax.sharding import PartitionSpec as P

HD = 128
SPAN = 64
NEIGH = 2
RETR = 128


masked_score = -1e30


def passed_along(value, axis, steps):
    count = lax.axis_size(axis)
    leading, last = (max(0, -steps), min(count, count - steps))
    return lax.ppermute(value, axis, [(source, source + steps) for source in range(leading, last)])


def fold_block(carry_state, query_rows, query_pos, key_rows, value_rows, key_pos, score_scale):
    summed, running_max, totals = carry_state
    scores = (
        jnp.einsum("qhe,khe->hqk", query_rows, key_rows, preferred_element_type=jnp.float32)
        * score_scale
    )
    allowed = (key_pos[None, :] <= query_pos[:, None])[None]
    scores = jnp.where(allowed, scores, masked_score)
    new_max = jnp.maximum(running_max, jnp.max(scores, axis=2))
    weights = jnp.where(allowed, jnp.exp(scores - new_max[:, :, None]), 0.0)
    totals = jnp.sum(weights, axis=2)
    summed = jnp.einsum(
        "hqk,khe->hqe", weights.astype(jnp.bfloat16), value_rows, preferred_element_type=jnp.float32
    )
    return (summed, new_max, totals)


def empty_state(heads_here, row_total):
    return (
        jnp.zeros((heads_here, row_total, HD), jnp.float32),
        jnp.full((heads_here, row_total), masked_score, jnp.float32),
        jnp.zeros((heads_here, row_total), jnp.float32),
    )


def finish_state(carry_state):
    summed, running_max, totals = carry_state
    normed = summed / totals[:, :, None]
    return jnp.transpose(normed, (1, 0, 2)).reshape(
        normed.shape[1], normed.shape[0] * normed.shape[2]
    )


def per_device(queries, keys, values, cross_queries, neighbour_ids, database, out_weight):
    row_count = queries.shape[1]
    feat_here = queries.shape[2]
    heads_here = feat_here // HD
    score_scale = 1.0 / math.sqrt(HD)
    seq_index = lax.axis_index("seq")
    own_first = seq_index * row_count
    own_pos = own_first + jnp.arange(row_count, dtype=jnp.int32)
    query_rows = queries[0].reshape(row_count, heads_here, HD)
    groups_list = [(query_rows, own_pos)]
    start_states = tuple(
        (empty_state(heads_here, group_pos.shape[0]) for group_rows, group_pos in groups_list)
    )
    key_block = lax.all_gather(keys, "seq", axis=1, tiled=True)[0]
    block_rows = key_block.shape[0]
    key_rows = key_block.reshape(block_rows, heads_here, HD)
    value_rows = lax.all_gather(values, "seq", axis=1, tiled=True)[0].reshape(
        block_rows, heads_here, HD
    )
    key_pos = jnp.arange(block_rows, dtype=jnp.int32)
    updated = []
    for carry_state, (group_rows, group_pos) in zip(start_states, groups_list):

        def visit_block(kept_state, group_rows=group_rows, group_pos=group_pos):
            return fold_block(
                kept_state, group_rows, group_pos, key_rows, value_rows, key_pos, score_scale
            )

        updated.append(visit_block(carry_state))
    states = tuple(updated)
    self_out = finish_state(states[0])
    id_pairs = neighbour_ids[0].reshape(-1, 2)
    shard_of = id_pairs[:, 0]
    block_of = id_pairs[:, 1]
    spans_here = neighbour_ids.shape[1]
    every_shard = lax.all_gather(database, "dp", axis=0, tiled=True)
    fetched = jnp.stack([every_shard[shard_of, 0, block_of], every_shard[shard_of, 1, block_of]])
    neighbour_rows = NEIGH * RETR
    grouped = fetched.reshape(2, spans_here, neighbour_rows, heads_here, HD)
    previous = passed_along(grouped[:, spans_here - 1], "seq", 1)
    extended = jnp.concatenate([previous[:, None], grouped], axis=1)
    padded = jnp.concatenate(
        [
            jnp.zeros((1, feat_here), jnp.bfloat16),
            cross_queries[0],
            jnp.zeros((SPAN - 1, feat_here), jnp.bfloat16),
        ],
        axis=0,
    )
    padded = padded.reshape(spans_here + 1, SPAN, heads_here, HD)
    scores = (
        jnp.einsum("gqhe,gkhe->ghqk", padded, extended[0], preferred_element_type=jnp.float32)
        * score_scale
    )
    row_max = jnp.max(scores, axis=3, keepdims=True)
    weights = jnp.exp(scores - row_max)
    totals = jnp.sum(weights, axis=3)
    summed_cross = jnp.einsum(
        "ghqk,gkhe->gqhe",
        weights.astype(jnp.bfloat16),
        extended[1],
        preferred_element_type=jnp.float32,
    )
    cross_out = summed_cross / jnp.transpose(totals, (0, 2, 1))[:, :, :, None]
    valid = ((jnp.arange(spans_here + 1) > 0) | (seq_index > 0)).astype(jnp.float32)
    cross_out = cross_out * valid[:, None, None, None]
    cross_out = cross_out.reshape((spans_here + 1) * SPAN, feat_here)[1 : 1 + row_count]
    attended = (self_out + cross_out).astype(jnp.bfloat16)
    own_sums = lax.psum_scatter(
        lax.dot_general(
            out_weight, attended, (((0,), (1,)), ((), ())), preferred_element_type=jnp.float32
        ).astype(jnp.bfloat16),
        "mp",
        scatter_dimension=0,
        tiled=True,
    )
    return jnp.transpose(own_sums)[None]


def solution(mesh):
    placed = (
        P("dp", "seq", "mp"),
        P("dp", "seq", "mp"),
        P("dp", "seq", "mp"),
        P("dp", "seq", "mp"),
        P("dp", "seq", None, None),
        P("dp", None, None, None, "mp"),
        P("mp", None),
    )
    return jax.shard_map(
        per_device, mesh=mesh, in_specs=placed, out_specs=P("dp", "seq", "mp"), check_vma=False
    )
```

profile of v0, /device:TPU:8, one launch (start us, length us, event | category | flops | bytes accessed | tf_op | source)
XLA Modules:
  0.0 206.7 jit_solution(13058635639013347483)
XLA Ops:
  6.5 0.7 all-gather.6.cloned.1.call-update
  7.3 0.7 all-gather.8.cloned.1.call-update
  8.1 0.8 copy.23
  9.7 0.7 copy.38
  10.4 0.7 iota_compare_fusion
  11.1 26.9 %all-gather.6.cloned.1.call-done = bf16[1,512,1024]{2,1,0:T(8,128)(2,1)} async-done(((bf16[1,128,1024]{2,1,0:T(8,128)(2,1)}), bf16[1,512,1024]{2,1,0:T(8,128)(2,1)}) %all-gather.6.cloned.1.call-update) | async-done | bytes 1048592 | tf_op jit(solution)/shard_map/all_gather | solution.py:72
  38.0 2.3 %copy.26 = bf16[1,512,1024]{1,2,0:T(8,128)(2,1)} copy(bf16[1,512,1024]{2,1,0:T(8,128)(2,1)} %all-gather.6.cloned.1.call-done) | data formatting | bytes 2097152 | tf_op jit(solution)/shard_map/all_gather | solution.py:72
  40.3 81.0 %all-gather.8.cloned.1.call-done = bf16[4,2,6,128,1024]{4,3,2,1,0:T(8,128)(2,1)} async-done(((bf16[1,2,6,128,1024]{4,3,2,1,0:T(8,128)(2,1)}), bf16[4,2,6,128,1024]{4,3,2,1,0:T(8,128)(2,1)}) %all-gather.8.cloned.1.call-update) | async-done | bytes 12582928 | tf_op jit(solution)/shard_map/all_gather | solution.py:91
  121.2 5.2 %gather_fusion = bf16[4,128,1024]{2,1,0:T(8,128)(2,1)S(1)} fusion(bf16[4,2,6,128,1024]{4,3,2,1,0:T(8,128)(2,1)} %all-gather.8.cloned.1.call-done, s32[4]{0:T(128)S(1)} %get-tuple-element.8), kind=kCustom, calls=%fused_computation | custom fusion | bytes 2097200 | tf_op jit(solution)/shard_map/gather | solution.py:92
  126.7 5.4 %gather_fusion.1 = bf16[4,128,1024]{2,1,0:T(8,128)(2,1)S(1)} fusion(bf16[4,2,6,128,1024]{4,3,2,1,0:T(8,128)(2,1)} %all-gather.8.cloned.1.call-done, s32[4]{0:T(128)S(1)} %get-tuple-element.7), kind=kCustom, calls=%fused_computation.1 | custom fusion | bytes 2097200 | tf_op jit(solution)/shard_map/gather | solution.py:92
  132.6 0.3 copy_dynamic-update-slice_fusion
  132.9 1.0 slice_bitcast_fusion
  133.9 3.4 %collective-permute-start = (bf16[2,256,8,128]{3,1,2,0:T(8,128)(2,1)}, bf16[2,256,8,128]{3,1,2,0:T(8,128)(2,1)}, u32[]{:S(2)}, u32[]{:S(2)}) collective-permute-start(bf16[2,256,8,128]{3,1,2,0:T(8,128)(2,1)} %slice_bitcast_fusion), channel_id=1, source_target_pairs={{0,2},{2,4},{4,6},{1,3},{3,5},{5,7},{8,10},{10,12},{12,14},{9,11},... | collective-permute-start | bytes 3145736 | tf_op jit(solution)/shard_map/ppermute | solution.py:20
  137.3 23.7 %all-gather.4.cloned.1.call-done = bf16[1,512,1024]{1,2,0:T(8,128)(2,1)} async-done(((bf16[1,128,1024]{1,2,0:T(8,128)(2,1)}), bf16[1,512,1024]{1,2,0:T(8,128)(2,1)}) %all-gather.4.cloned.1.call-update) | async-done | bytes 1048592 | tf_op jit(solution)/shard_map/all_gather | solution.py:69
  161.0 1.9 fusion.1
  162.9 0.7 fusion.13
  163.6 0.8 fusion.26
  164.6 7.5 %collective-permute-done = bf16[2,256,8,128]{3,1,2,0:T(8,128)(2,1)} collective-permute-done((bf16[2,256,8,128]{3,1,2,0:T(8,128)(2,1)}, bf16[2,256,8,128]{3,1,2,0:T(8,128)(2,1)}, u32[]{:S(2)}, u32[]{:S(2)}) %collective-permute-start) | collective-permute-done | bytes 1048608 | tf_op jit(solution)/shard_map/ppermute | solution.py:20
  172.2 1.9 fusion.50
  174.1 0.5 fusion.15
  174.7 1.8 fusion.23
  176.5 0.5 copy.32
  177.1 2.3 %fusion = bf16[4096,128]{0,1:T(8,128)(2,1)} fusion(bf16[1024,4096]{1,0:T(8,128)(2,1)S(1)} %bitcast.72, f32[128,1024]{1,0:T(8,128)S(1)} %copy.33, f32[192,1024]{1,0:T(8,128)S(1)} %bitcast.77), kind=kOutput, calls=%fused_computation.3 | convolution fusion | flops 1074528256 | bytes 10485760 | tf_op jit(solution)/shard_map/dot_general | solution.py:125
  179.5 20.7 %reduce-scatter.2.cloned.1.call-done = bf16[2048,128]{0,1:T(8,128)(2,1)} async-done(((bf16[4096,128]{0,1:T(8,128)(2,1)}), bf16[2048,128]{0,1:T(8,128)(2,1)}) %reduce-scatter.2.cloned.1.call-update) | async-done | bytes 524304 | tf_op jit(solution)/shard_map/reduce_scatter | solution.py:124
  (42 shorter events, 1.9 us)
Async XLA Ops:
  6.5 1.5 copy-start.4
  6.5 2.6 %copy-start.3 = (bf16[1,128,1024]{2,1,0:T(8,128)(2,1)S(1)}, bf16[1,128,1024]{2,1,0:T(8,128)(2,1)}, u32[]{:S(2)}) copy-start(bf16[1,128,1024]{2,1,0:T(8,128)(2,1)} %param.10) | copy-start | bytes 786436
  6.5 31.5 %all-gather.6.cloned.1.call-start = ((), (), s32[]{:S(2)}) async-start(), calls=%async_computation.2 | async-start | bytes 1310720 | tf_op jit(solution)/shard_map/all_gather | solution.py:72
  7.3 2.0 copy-start.6
  7.3 2.4 %copy-start.5 = (bf16[1,128,1024]{2,1,0:T(8,128)(2,1)S(1)}, bf16[1,128,1024]{2,1,0:T(8,128)(2,1)}, u32[]{:S(2)}) copy-start(bf16[1,128,1024]{2,1,0:T(8,128)(2,1)} %param.7) | copy-start | bytes 786436
  7.3 114.0 %all-gather.8.cloned.1.call-start = ((), (), s32[]{:S(2)}) async-start(), calls=%async_computation.3 | async-start | bytes 15728640 | tf_op jit(solution)/shard_map/all_gather | solution.py:91
  8.0 153.0 %all-gather.4.cloned.1.call-start = ((), (), s32[]{:S(2)}) async-start(), calls=%async_computation.1 | async-start | bytes 1310720 | tf_op jit(solution)/shard_map/all_gather | solution.py:69
  9.0 191.2 %reduce-scatter.2.cloned.1.call-start = ((), (), s32[]{:S(2)}) async-start(), calls=%async_computation.4 | async-start | bytes 1572864 | tf_op jit(solution)/shard_map/reduce_scatter | solution.py:124
  132.6 28.5 %copy-start.1 = (bf16[16,8,8,128]{3,2,1,0:T(8,128)(2,1)S(1)}, bf16[16,8,8,128]{3,2,1,0:T(8,128)(2,1)}, u32[]{:S(2)}) copy-start(bf16[16,8,8,128]{3,2,1,0:T(8,128)(2,1)} %copy.38) | copy-start | bytes 786436
  132.6 28.4 %copy-start.2 = (pred[128,512]{1,0:T(8,128)(4,1)S(1)}, pred[128,512]{1,0:T(8,128)(4,1)}, u32[]{:S(2)}) copy-start(pred[128,512]{1,0:T(8,128)(4,1)} %iota_compare_fusion) | copy-start | bytes 196612
  133.9 38.2 %collective-permute-start = (bf16[2,256,8,128]{3,1,2,0:T(8,128)(2,1)}, bf16[2,256,8,128]{3,1,2,0:T(8,128)(2,1)}, u32[]{:S(2)}, u32[]{:S(2)}) collective-permute-start(bf16[2,256,8,128]{3,1,2,0:T(8,128)(2,1)} %slice_bitcast_fusion), channel_id=1, source_target_pairs={{0,2},{2,4},{4,6},{1,3},{3,5},{5,7},{8,10},{10,12},{12,14},{9,11},... | collective-permute-start | bytes 3145736 | tf_op jit(solution)/shard_map/ppermute | solution.py:20
  161.0 2.6 %copy-start = (bf16[1,512,1024]{1,2,0:T(8,128)(2,1)S(1)}, bf16[1,512,1024]{1,2,0:T(8,128)(2,1)}, u32[]{:S(2)}) copy-start(bf16[1,512,1024]{1,2,0:T(8,128)(2,1)} %copy.26) | copy-start | bytes 3145732
  172.2 4.9 %slice-start = ((s8[8388608]{0:T(1024)(128)(4,1)}), s8[4194304]{0:T(1024)(128)(4,1)S(1)}, s32[]{:S(2)}) async-start(s8[8388608]{0:T(1024)(128)(4,1)} %bitcast.71), calls=%async_computation.5 | async-start | bytes 8388608
  174.6 2.5 %slice-start.1 = ((s8[8388608]{0:T(1024)(128)(4,1)}), s8[4194304]{0:T(1024)(128)(4,1)S(1)}, s32[]{:S(2)}) async-start(s8[8388608]{0:T(1024)(128)(4,1)} %bitcast.71), calls=%async_computation.6 | async-start | bytes 8388608
Sparse Core Ops, SparseCore 0:
  8.9 29.0 all-gather.5
  39.6 81.6 all-gather.7
  122.8 38.1 all-gather.3
  179.6 20.5 reduce-scatter.1
where the time goes:
time: 209 us; the launch traced here: 207 us
  waiting for transfers between devices  161 us (77%)
  local copies, waits for them, and re-layouts  17.7 us (8%)
  between operations  13.4 us (6%)
  matrix products  8.72 us (4%)
  starting transfers between devices  3.5 us (2%)
  other arithmetic  2.16 us (1%)
    all_gather x1, waiting for transfers between devices, per_device(): every_shard = lax.all_gather(database, 'dp', axis=0, tiled=True)  81 us
    all_gather x1, waiting for transfers between devices, per_device(): lax.all_gather(values, 'seq', axis=1, tiled=True)[0]  26.9 us
    all_gather x1, waiting for transfers between devices, per_device(): key_block = lax.all_gather(keys, 'seq', axis=1, tiled=True)[0]  23.7 us
    reduce_scatter x1, waiting for transfers between devices, per_device(): lax.psum_scatter(lax.dot_general(out_weight, attended, (((0,), (1,)), (()...  20.7 us
    ppermute x1, waiting for transfers between devices, passed_along(): lax.ppermute(value, axis, [(source, source + steps) for source in range(l...  7.53 us
    gather x1, local copies, waits for them, and re-layouts, per_device(): every_shard[shard_of, 1, block_of]  5.38 us
    gather x1, local copies, waits for them, and re-layouts, per_device(): every_shard[shard_of, 0, block_of]  5.19 us
  transfers between devices with their start and end apart: 5, of which 5 were waited for; matrix products, arithmetic and copies ran while one was open for 10% of the time, Pallas kernels for 0%

commit v1 on v0

--- a/solution.py
+++ b/solution.py
@@ -1,8 +1,11 @@
+import functools
 import math
 
 import jax
 import jax.numpy as jnp
 from jax import lax
+from jax.experimental import pallas as pl
+from jax.experimental.pallas import tpu as pltpu
 from jax.sharding import PartitionSpec as P
 
 HD = 128
@@ -131,6 +134,419 @@
     )
     return jnp.transpose(own_sums)[None]
 
+NEG = -1e30
+LOG2E = 1.4426950408889634
+PAIR = 2 * HD
+PIECE = PAIR + 16
+TILE = 512
+MESH = pl.DeviceIdType.MESH
+
+
+def nt_dot(a, b):
+    return lax.dot_general(a, b, (((1,), (1,)), ((), ())), preferred_element_type=jnp.float32)
+
+
+def tn_dot(a, b):
+    return lax.dot_general(a, b, (((0,), (0,)), ((), ())), preferred_element_type=jnp.float32)
+
+
+def pack_piece(parts):
+    row = lax.broadcasted_iota(jnp.int32, (16, HD), 0)
+    stats = jnp.zeros((16, HD), jnp.float32)
+    for index, (_, lse) in enumerate(parts):
+        rest = lse
+        for term in range(3):
+            rounded = rest.astype(jnp.bfloat16).astype(jnp.float32)
+            stats = jnp.where(row == 3 * index + term, rounded, stats)
+            rest = rest - rounded
+    return jnp.concatenate(
+        [parts[0][0].astype(jnp.bfloat16), parts[1][0].astype(jnp.bfloat16), stats.astype(jnp.bfloat16)],
+        axis=0,
+    )
+
+
+def attend_pair(q, k, v, scale, allowed=None):
+    parts = []
+    for h in range(2):
+        cols = slice(h * HD, (h + 1) * HD)
+        scores = nt_dot(k[:, cols], q[:, cols]) * scale
+        if allowed is not None:
+            scores = jnp.where(allowed, scores, NEG)
+        top = jnp.max(scores, axis=0, keepdims=True)
+        weights = jnp.exp2(scores - top)
+        total = jnp.sum(weights, axis=0, keepdims=True)
+        summed = tn_dot(v[:, cols], weights.astype(jnp.bfloat16)) / total
+        parts.append((summed, top + jnp.log2(total)))
+    return pack_piece(parts)
+
+
+def cross_pair(q, keys, vals, owned, in_first, in_last, scale):
+    parts = []
+    for h in range(2):
+        cols = slice(h * HD, (h + 1) * HD)
+        qh = q[:, cols]
+        s0, s1, s2 = [nt_dot(k[:, cols], qh) for k in keys]
+        scores = jnp.where(in_first, s0, jnp.where(in_last, s2, s1)) * scale
+        scores = jnp.where(owned, scores, NEG)
+        top = jnp.max(scores, axis=0, keepdims=True)
+        weights = jnp.where(owned, jnp.exp2(scores - top), 0.0)
+        total = jnp.sum(weights, axis=0, keepdims=True)
+        some = total > 0.0
+        safe = jnp.where(some, total, 1.0)
+        low = weights.astype(jnp.bfloat16)
+        o0, o1, o2 = [tn_dot(v[:, cols], low) for v in vals]
+        summed = jnp.where(in_first, o0, jnp.where(in_last, o2, o1)) / safe
+        parts.append((summed, jnp.where(some, top + jnp.log2(safe), NEG)))
+    return pack_piece(parts)
+
+
+def merge_pieces(pieces, h):
+    lses = []
+    for piece in pieces:
+        stats = piece[PAIR:, :].astype(jnp.float32)
+        lses.append(stats[3 * h : 3 * h + 1] + stats[3 * h + 1 : 3 * h + 2] + stats[3 * h + 2 : 3 * h + 3])
+    top = functools.reduce(jnp.maximum, lses)
+    shares = [jnp.exp2(lse - top) for lse in lses]
+    total = functools.reduce(jnp.add, shares)
+    summed = 0.0
+    for piece, share in zip(pieces, shares):
+        summed = summed + piece[h * HD : (h + 1) * HD, :].astype(jnp.float32) * (share / total)
+    return summed
+
+
+def layer_kernel(
+    q, k, v, cq, ids, db_hbm, w_hbm, out,
+    db, w, kv0, qin, cqin, sp, stx, cp, ctx, att, ptx, prx, ids_tx, ids_rx, ids_s,
+    db_sem, w_sem, ids_sem, kv_ss, kv_rs, q_ss, q_rs, cq_ss, cq_rs, sp_ss, sp_rs, cp_ss, cp_rs,
+    i1_ss, i1_rs, i2_ss, i2_rs, p_ss, p_rs,
+):
+    d = lax.axis_index("dp")
+    s = lax.axis_index("seq")
+    m = lax.axis_index("mp")
+    dps = cqin.shape[0]
+    chunks = cqin.shape[1]
+    rows = q.shape[0]
+    half = out.shape[1]
+    tiles = half // TILE
+    scale = LOG2E / math.sqrt(HD)
+    other = 1 - m
+
+    def cols_of(c):
+        return pl.ds(pl.multiple_of(c * PAIR, PAIR), PAIR)
+
+    def remote(src, dst, ss, rs, **where):
+        return pltpu.make_async_remote_copy(
+            src_ref=src, dst_ref=dst, send_sem=ss, recv_sem=rs, device_id=where, device_id_type=MESH
+        )
+
+    db_copy = pltpu.make_async_copy(db_hbm, db, db_sem)
+    db_copy.start()
+    w_copies = [
+        pltpu.make_async_copy(
+            w_hbm.at[:, pl.ds(pl.multiple_of(side * half, TILE), half)], w.at[i], w_sem.at[i]
+        )
+        for i, side in enumerate((other, m))
+    ]
+
+    barrier = pltpu.get_barrier_semaphore()
+    for j in range(1, dps):
+        pl.semaphore_signal(barrier, inc=1, device_id={"dp": lax.rem(d + j, dps)}, device_id_type=MESH)
+    for j in range(1, 4):
+        pl.semaphore_signal(barrier, inc=1, device_id={"seq": lax.rem(s + j, 4)}, device_id_type=MESH)
+    pl.semaphore_signal(barrier, inc=1, device_id={"mp": other}, device_id_type=MESH)
+    pl.semaphore_wait(barrier, dps + 3)
+
+    def id_hop():
+        return remote(ids, ids_tx.at[1], i1_ss, i1_rs, seq=lax.rem(s + 1, 4))
+
+    def kv_hop(c, which):
+        return remote((k, v)[which].at[:, cols_of(c)], kv0.at[c, which], kv_ss.at[c, which], kv_rs.at[c, which], seq=1)
+
+    def q_hop(c, dest):
+        slot = jnp.maximum(s - 2, 0)
+        return remote(q.at[:, cols_of(c)], qin.at[slot, c], q_ss.at[dest - 1, c], q_rs.at[slot, c], seq=dest)
+
+    def q_arrived(c, slot):
+        remote(q.at[:, cols_of(c)], qin.at[slot, c], q_ss.at[0, c], q_rs.at[slot, c], seq=1).wait_recv()
+
+    def cq_hop(c, j):
+        return remote(
+            cq.at[:, cols_of(c)], cqin.at[j, c], cq_ss.at[j, c], cq_rs.at[j, c], dp=lax.rem(d + j, dps)
+        )
+
+    def sp_hop(c, slot, dest, place):
+        return remote(stx.at[slot, c], sp.at[place, c], sp_ss.at[slot, c], sp_rs.at[place, c], seq=dest)
+
+    def cp_hop(c, j):
+        return remote(
+            ctx.at[j, c], cp.at[j, c], cp_ss.at[j, c], cp_rs.at[j, c], dp=lax.rem(d - j + dps, dps)
+        )
+
+    def id_share(j):
+        return remote(ids_tx, ids_rx.at[j], i2_ss.at[j], i2_rs.at[j], dp=lax.rem(d + j, dps))
+
+    def p_hop(t):
+        return remote(ptx.at[t], prx.at[t], p_ss.at[t], p_rs.at[t], mp=other)
+
+    @pl.when(s < 3)
+    def _():
+        id_hop().start()
+
+    @pl.loop(0, chunks)
+    def _(c):
+        @pl.when(s == 0)
+        def _():
+            kv_hop(c, 0).start()
+            kv_hop(c, 1).start()
+
+        @pl.when(s >= 2)
+        def _():
+            q_hop(c, 1).start()
+
+        @pl.when(s == 3)
+        def _():
+            q_hop(c, 2).start()
+
+        @pl.loop(1, dps)
+        def _(j):
+            cq_hop(c, j).start()
+
+        cqin[0, c] = cq[:, cols_of(c)]
+
+    for copy in w_copies:
+        copy.start()
+
+    ids_tx[0] = ids[...]
+
+    @pl.when(s == 0)
+    def _():
+        ids_tx[1] = jnp.zeros_like(ids)
+
+    @pl.when(s > 0)
+    def _():
+        id_hop().wait_recv()
+
+    for j in range(1, dps):
+        id_share(j).start()
+    ids_rx[0] = ids_tx[...]
+
+    neutral = jnp.concatenate(
+        [jnp.zeros((PAIR, HD), jnp.bfloat16), jnp.full((16, HD), NEG, jnp.bfloat16)], axis=0
+    )
+    key_at = lax.broadcasted_iota(jnp.int32, (rows, HD), 0)
+    query_at = lax.broadcasted_iota(jnp.int32, (rows, HD), 1)
+    causal = key_at <= query_at
+
+    @pl.loop(0, chunks)
+    def _(c):
+        cols = cols_of(c)
+        sp[0, c] = attend_pair(q[:, cols], k[:, cols], v[:, cols], scale, causal)
+
+        @pl.when(s < 1)
+        def _():
+            sp[1, c] = neutral
+
+        @pl.when(s < 3)
+        def _():
+            sp[2, c] = neutral
+
+    for j in range(1, dps):
+        id_share(j).wait_recv()
+    ids_copy = pltpu.make_async_copy(ids_rx, ids_s, ids_sem)
+    ids_copy.start()
+    ids_copy.wait()
+    db_copy.wait()
+
+    lane = lax.broadcasted_iota(jnp.int32, (1, HD), 1)
+    in_first = lane < SPAN - 1
+    in_last = lane == 2 * SPAN - 1
+    live = jnp.logical_or(lane >= SPAN - 1, s > 0)
+
+    @pl.loop(0, chunks)
+    def _(c):
+        cols = cols_of(c)
+
+        @pl.when(s == 1)
+        def _():
+            kv_hop(c, 0).wait_recv()
+            kv_hop(c, 1).wait_recv()
+            k0 = kv0[c, 0]
+            v0 = kv0[c, 1]
+            sp[1, c] = attend_pair(q[:, cols], k0, v0, scale)
+
+            @pl.loop(0, 2)
+            def _(slot):
+                q_arrived(c, slot)
+                both_k = jnp.concatenate([kv0[c, 0], k[:, cols]], axis=0)
+                both_v = jnp.concatenate([kv0[c, 1], v[:, cols]], axis=0)
+                stx[slot, c] = attend_pair(qin[slot, c], both_k, both_v, scale)
+                sp_hop(c, slot, 2 + slot, 1).start()
+
+        @pl.when(s == 2)
+        def _():
+            q_arrived(c, 1)
+            stx[1, c] = attend_pair(qin[1, c], k[:, cols], v[:, cols], scale)
+            sp_hop(c, 1, 3, 2).start()
+
+        @pl.loop(0, dps)
+        def _(turn):
+            j = lax.rem(turn + 1, dps)
+
+            @pl.when(j > 0)
+            def _():
+                cq_hop(c, j).wait_recv()
+
+            keys, vals, shards = [], [], []
+            for which, span in ((1, 1), (0, 0), (0, 1)):
+                blocks = [ids_s[j, which, 0, span * 4 + n * 2 + 1] for n in range(NEIGH)]
+                shards.append([ids_s[j, which, 0, span * 4 + n * 2] for n in range(NEIGH)])
+                keys.append(jnp.concatenate([db[0, b, :, cols] for b in blocks], axis=0))
+                vals.append(jnp.concatenate([db[1, b, :, cols] for b in blocks], axis=0))
+            owned = []
+            for n in range(NEIGH):
+                shard = jnp.where(in_first, shards[0][n], jnp.where(in_last, shards[2][n], shards[1][n]))
+                row = jnp.where(jnp.logical_and(shard == d, live), 1, 0)
+                owned.append(jnp.broadcast_to(row, (RETR, HD)))
+            owned = jnp.concatenate(owned, axis=0) > 0
+            ctx[j, c] = cross_pair(cqin[j, c], keys, vals, owned, in_first, in_last, scale)
+
+            @pl.when(j > 0)
+            def _():
+                cp_hop(c, j).start()
+
+    @pl.loop(0, chunks)
+    def _(c):
+        @pl.when(s >= 2)
+        def _():
+            sp_hop(c, 0, 2, 1).wait_recv()
+
+        @pl.when(s == 3)
+        def _():
+            sp_hop(c, 0, 3, 2).wait_recv()
+
+        for j in range(1, dps):
+            cp_hop(c, j).wait_recv()
+        self_pieces = [sp[i, c] for i in range(3)]
+        cross_pieces = [ctx[0, c]] + [cp[j, c] for j in range(1, dps)]
+        for h in range(2):
+            both = merge_pieces(self_pieces, h) + merge_pieces(cross_pieces, h)
+            att[:, pl.ds(pl.multiple_of(c * PAIR + h * HD, HD), HD)] = both.T.astype(jnp.bfloat16)
+
+    def tile_cols(t):
+        return pl.ds(pl.multiple_of(t * TILE, TILE), TILE)
+
+    w_copies[0].wait()
+
+    @pl.loop(0, tiles)
+    def _(t):
+        ptx[t] = jnp.dot(
+            att[...], w[0, :, tile_cols(t)], preferred_element_type=jnp.float32
+        ).astype(jnp.bfloat16)
+        p_hop(t).start()
+
+    w_copies[1].wait()
+
+    @pl.loop(0, tiles)
+    def _(t):
+        own = jnp.dot(att[...], w[1, :, tile_cols(t)], preferred_element_type=jnp.float32)
+        p_hop(t).wait_recv()
+        out[:, tile_cols(t)] = (own + prx[t].astype(jnp.float32)).astype(jnp.bfloat16)
+
+    @pl.when(s < 3)
+    def _():
+        id_hop().wait_send()
+
+    for j in range(1, dps):
+        id_share(j).wait_send()
+
+    @pl.loop(0, chunks)
+    def _(c):
+        @pl.when(s == 0)
+        def _():
+            kv_hop(c, 0).wait_send()
+            kv_hop(c, 1).wait_send()
+
+        @pl.when(s >= 2)
+        def _():
+            q_hop(c, 1).wait_send()
+
+        @pl.when(s == 3)
+        def _():
+            q_hop(c, 2).wait_send()
+
+        @pl.when(s == 1)
+        def _():
+            sp_hop(c, 0, 2, 1).wait_send()
+            sp_hop(c, 1, 3, 1).wait_send()
+
+        @pl.when(s == 2)
+        def _():
+            sp_hop(c, 1, 3, 2).wait_send()
+
+        @pl.loop(1, dps)
+        def _(j):
+            cq_hop(c, j).wait_send()
+            cp_hop(c, j).wait_send()
+
+    @pl.loop(0, tiles)
+    def _(t):
+        p_hop(t).wait_send()
+
+
+def fused_device(queries, keys, values, cross_queries, neighbour_ids, database, out_weight):
+    rows, feat = queries.shape[1:]
+    dps = lax.axis_size("dp")
+    chunks = feat // PAIR
+    width = out_weight.shape[1]
+    half = width // 2
+    tiles = half // TILE
+    ids = neighbour_ids.reshape(1, -1)
+    ids = jnp.pad(ids, ((0, 7), (0, 128 - ids.shape[1])))
+    bf16 = jnp.bfloat16
+    dma = pltpu.SemaphoreType.DMA
+    vmem = pl.BlockSpec(memory_space=pltpu.VMEM)
+    anywhere = pl.BlockSpec(memory_space=pl.ANY)
+    scratch = [
+        pltpu.VMEM(database.shape[1:], bf16),
+        pltpu.VMEM((2, feat, half), bf16),
+        pltpu.VMEM((chunks, 2, rows, PAIR), bf16),
+        pltpu.VMEM((2, chunks, rows, PAIR), bf16),
+        pltpu.VMEM((dps, chunks, rows, PAIR), bf16),
+        pltpu.VMEM((3, chunks, PIECE, rows), bf16),
+        pltpu.VMEM((2, chunks, PIECE, rows), bf16),
+        pltpu.VMEM((dps, chunks, PIECE, rows), bf16),
+        pltpu.VMEM((dps, chunks, PIECE, rows), bf16),
+        pltpu.VMEM((rows, feat), bf16),
+        pltpu.VMEM((tiles, rows, TILE), bf16),
+        pltpu.VMEM((tiles, rows, TILE), bf16),
+        pltpu.VMEM((2, 8, 128), jnp.int32),
+        pltpu.VMEM((dps, 2, 8, 128), jnp.int32),
+        pltpu.SMEM((dps, 2, 8, 128), jnp.int32),
+        dma, dma((2,)), dma,
+        dma((chunks, 2)), dma((chunks, 2)),
+        dma((2, chunks)), dma((2, chunks)),
+        dma((dps, chunks)), dma((dps, chunks)),
+        dma((2, chunks)), dma((3, chunks)),
+        dma((dps, chunks)), dma((dps, chunks)),
+        dma, dma, dma((dps,)), dma((dps,)),
+        dma((tiles,)), dma((tiles,)),
+    ]
+    flops = 2 * rows * feat * width + 2 * 2 * rows * feat * (8 * rows + dps * 6 * RETR)
+    result = pl.pallas_call(
+        layer_kernel,
+        out_shape=jax.ShapeDtypeStruct((rows, half), bf16),
+        in_specs=[vmem] * 5 + [anywhere] * 2,
+        out_specs=vmem,
+        scratch_shapes=scratch,
+        compiler_params=pltpu.CompilerParams(
+            collective_id=0, has_side_effects=True, vmem_limit_bytes=50 * 1024 * 1024
+        ),
+        cost_estimate=pl.CostEstimate(
+            flops=flops, bytes_accessed=2 * (feat * width + database.size), transcendentals=0
+        ),
+    )(queries[0], keys[0], values[0], cross_queries[0], ids, database[0], out_weight)
+    return result[None]
+
 
 def solution(mesh):
     placed = (
@@ -142,6 +558,11 @@
         P("dp", None, None, None, "mp"),
         P("mp", None),
     )
+    fits = mesh.shape["seq"] == 4 and mesh.shape["mp"] == 2
     return jax.shard_map(
-        per_device, mesh=mesh, in_specs=placed, out_specs=P("dp", "seq", "mp"), check_vma=False
-    )
+        fused_device if fits else per_device,
+        mesh=mesh,
+        in_specs=placed,
+        out_specs=P("dp", "seq", "mp"),
+        check_vma=False,
+    )

time: 209 us -> 59.5 us (0.28)
  waiting for transfers between devices: 161 us -> 0 us
  Pallas kernels: 0 us -> 53.9 us
  between operations: 13.4 us -> 0.01 us
  local copies, waits for them, and re-layouts: 17.7 us -> 5.36 us
  matrix products: 8.72 us -> 0 us
  starting transfers between devices: 3.5 us -> 0 us
  other arithmetic: 2.16 us -> 0 us
    all_gather x3 -> x0, waiting for transfers between devices: 132 us -> none  [the longest x1 81 us: per_device(): every_shard = lax.all_gather(database, 'dp', axis=0, tiled=True)]
    pallas_call x0 -> x1, Pallas kernels: none -> 53.9 us  [fused_device(): pl.pallas_call(layer_kernel, out_shape=jax.ShapeDtypeStruct((rows, half),...]
    reduce_scatter x1 -> x0, waiting for transfers between devices: 20.7 us -> none  [per_device(): lax.psum_scatter(lax.dot_general(out_weight, attended, (((0,), (1,)), (()...]
    gather x2 -> x0, local copies, waits for them, and re-layouts: 10.6 us -> none  [the longest x1 5.38 us: per_device(): every_shard[shard_of, 1, block_of]]
    dot_general x5 -> x0, matrix products: 8.72 us -> none  [the longest x1 2.29 us: per_device(): lax.dot_general(out_weight, attended, (((0,), (1,)), ((), ())), preferred...]
    ppermute x1 -> x0, waiting for transfers between devices: 7.53 us -> none  [passed_along(): lax.ppermute(value, axis, [(source, source + steps) for source in range(l...]
    ppermute x1 -> x0, starting transfers between devices: 3.38 us -> none  [passed_along(): lax.ppermute(value, axis, [(source, source + steps) for source in range(l...]
    all_gather x1 -> x0, local copies, waits for them, and re-layouts: 2.26 us -> none  [per_device(): lax.all_gather(values, 'seq', axis=1, tiled=True)[0]]
  transfers between devices with their start and end apart: 5 -> 0, of which waited for: 5 -> 0; matrix products, arithmetic and copies ran while one was open for 10% -> 0% of each run, Pallas kernels for 0% -> 0%
where the time goes in v1:
time: 59.5 us; the launch traced here: 59.3 us
  Pallas kernels  53.9 us (91%)
  local copies, waits for them, and re-layouts  5.36 us (9%)
    pallas_call x1, Pallas kernels, fused_device(): pl.pallas_call(layer_kernel, out_shape=jax.ShapeDtypeStruct((rows, half),...  53.9 us
    unnamed x9, local copies, waits for them, and re-layouts  4.6 us

profile of v1, /device:TPU:8, one launch (start us, length us, event | category | flops | bytes accessed | tf_op | source)
XLA Modules:
  0.0 59.3 jit_solution(6457981184473442746)
XLA Ops:
  0.0 0.8 %reshape.3 = s32[1,8]{1,0:T(1,128)S(1)} reshape(s32[1,2,2,2]{3,2,1,0:T(2,128)} %param.11) | data formatting | bytes 64 | tf_op jit(solution)/shard_map/reshape | solution.py:503
  0.8 0.0 copy-start
  0.8 0.9 %copy-done = bf16[1,128,1024]{2,1,0:T(8,128)(2,1)S(1)} copy-done((bf16[1,128,1024]{2,1,0:T(8,128)(2,1)S(1)}, bf16[1,128,1024]{2,1,0:T(8,128)(2,1)}, u32[]{:S(2)}) %copy-start) | copy-done | bytes 262168
  1.7 0.0 copy-start.1
  1.7 0.9 %copy-done.1 = bf16[1,128,1024]{2,1,0:T(8,128)(2,1)S(1)} copy-done((bf16[1,128,1024]{2,1,0:T(8,128)(2,1)S(1)}, bf16[1,128,1024]{2,1,0:T(8,128)(2,1)}, u32[]{:S(2)}) %copy-start.1) | copy-done | bytes 262168
  2.7 0.0 copy-start.2
  2.7 0.9 %copy-done.2 = bf16[1,128,1024]{2,1,0:T(8,128)(2,1)S(1)} copy-done((bf16[1,128,1024]{2,1,0:T(8,128)(2,1)S(1)}, bf16[1,128,1024]{2,1,0:T(8,128)(2,1)}, u32[]{:S(2)}) %copy-start.2) | copy-done | bytes 262168
  3.6 0.0 copy-start.3
  3.6 0.9 %copy-done.3 = bf16[1,128,1024]{2,1,0:T(8,128)(2,1)S(1)} copy-done((bf16[1,128,1024]{2,1,0:T(8,128)(2,1)S(1)}, bf16[1,128,1024]{2,1,0:T(8,128)(2,1)}, u32[]{:S(2)}) %copy-start.3) | copy-done | bytes 262168
  4.6 53.9 %shard_map.73 = bf16[128,2048]{1,0:T(8,128)(2,1)S(1)} custom-call(bf16[128,1024]{1,0:T(8,128)(2,1)S(1)} %bitcast.7, bf16[128,1024]{1,0:T(8,128)(2,1)S(1)} %bitcast.8, bf16[128,1024]{1,0:T(8,128)(2,1)S(1)} %bitcast.9, bf16[128,1024]{1,0:T(8,128)(2,1)S(1)} %bitcast.10, s32[8,128]{1,0:T(8,128)S(1)} %pad.4.ids, bf16[2,6,128,1024]{3,2,1,0:T(8,128)(2,1)} %bitcast.11, ...), custom_call_target="tpu_custom_call" | custom-call | flops 3221225472 | bytes 11534336 | tf_op jit(solution)/shard_map/pallas_call | solution.py:535
  58.5 0.8 %copy.9 = bf16[1,128,2048]{2,1,0:T(8,128)(2,1)} copy(bf16[1,128,2048]{2,1,0:T(8,128)(2,1)S(1)} %bitcast.6) | data formatting | bytes 1048576
  (1 shorter events, 0.0 us)
Async XLA Ops:
  0.8 1.0 %copy-start = (bf16[1,128,1024]{2,1,0:T(8,128)(2,1)S(1)}, bf16[1,128,1024]{2,1,0:T(8,128)(2,1)}, u32[]{:S(2)}) copy-start(bf16[1,128,1024]{2,1,0:T(8,128)(2,1)} %param.7) | copy-start | bytes 786436
  1.7 0.9 %copy-start.1 = (bf16[1,128,1024]{2,1,0:T(8,128)(2,1)S(1)}, bf16[1,128,1024]{2,1,0:T(8,128)(2,1)}, u32[]{:S(2)}) copy-start(bf16[1,128,1024]{2,1,0:T(8,128)(2,1)} %param.8) | copy-start | bytes 786436
  2.7 0.9 %copy-start.2 = (bf16[1,128,1024]{2,1,0:T(8,128)(2,1)S(1)}, bf16[1,128,1024]{2,1,0:T(8,128)(2,1)}, u32[]{:S(2)}) copy-start(bf16[1,128,1024]{2,1,0:T(8,128)(2,1)} %param.9) | copy-start | bytes 786436
  3.6 0.9 %copy-start.3 = (bf16[1,128,1024]{2,1,0:T(8,128)(2,1)S(1)}, bf16[1,128,1024]{2,1,0:T(8,128)(2,1)}, u32[]{:S(2)}) copy-start(bf16[1,128,1024]{2,1,0:T(8,128)(2,1)} %param.10) | copy-start | bytes 786436

commit v2 on v1

--- a/solution.py
+++ b/solution.py
@@ -146,8 +146,8 @@
     return lax.dot_general(a, b, (((1,), (1,)), ((), ())), preferred_element_type=jnp.float32)
 
 
-def tn_dot(a, b):
-    return lax.dot_general(a, b, (((0,), (0,)), ((), ())), preferred_element_type=jnp.float32)
+def nn_dot(a, b):
+    return jnp.dot(a, b, preferred_element_type=jnp.float32)
 
 
 def pack_piece(parts):
@@ -165,38 +165,56 @@
     )
 
 
-def attend_pair(q, k, v, scale, allowed=None):
+def by_head(q):
+    blank = jnp.zeros((q.shape[0], HD), q.dtype)
+    return jnp.concatenate(
+        [
+            jnp.concatenate([q[:, :HD], blank], axis=1),
+            jnp.concatenate([blank, q[:, HD:]], axis=1),
+        ],
+        axis=0,
+    )
+
+
+def weigh(scores, scale):
+    top = jnp.max(scores, axis=0, keepdims=True)
+    weights = jnp.exp2((scores - top) * scale)
+    total = jnp.sum(weights, axis=0, keepdims=True)
+    return weights.astype(jnp.bfloat16), top, total
+
+
+def attend_pair(q, k, vt, scale, allowed=None):
+    scores = nt_dot(k, by_head(q))
+    if allowed is not None:
+        scores = jnp.where(allowed, scores, NEG)
+    low, top, total = weigh(scores, scale)
+    lse = top * scale + jnp.log2(total)
+    inverse = 1.0 / total
+    rows = q.shape[0]
     parts = []
     for h in range(2):
-        cols = slice(h * HD, (h + 1) * HD)
-        scores = nt_dot(k[:, cols], q[:, cols]) * scale
-        if allowed is not None:
-            scores = jnp.where(allowed, scores, NEG)
-        top = jnp.max(scores, axis=0, keepdims=True)
-        weights = jnp.exp2(scores - top)
-        total = jnp.sum(weights, axis=0, keepdims=True)
-        summed = tn_dot(v[:, cols], weights.astype(jnp.bfloat16)) / total
-        parts.append((summed, top + jnp.log2(total)))
+        lanes = slice(h * rows, (h + 1) * rows)
+        summed = nn_dot(vt[h * HD : (h + 1) * HD], low[:, lanes]) * inverse[:, lanes]
+        parts.append((summed, lse[:, lanes]))
     return pack_piece(parts)
 
 
-def cross_pair(q, keys, vals, owned, in_first, in_last, scale):
+def cross_pair(q, keys, vts, owned, in_first, in_last, scale):
+    both = by_head(q)
+    s0, s1, s2 = [nt_dot(k, both) for k in keys]
+    scores = jnp.where(in_first, s0, jnp.where(in_last, s2, s1))
+    scores = jnp.where(owned, scores, NEG)
+    low, top, total = weigh(scores, scale)
+    some = top > 0.5 * NEG
+    lse = jnp.where(some, top * scale + jnp.log2(total), NEG)
+    inverse = jnp.where(some, 1.0 / total, 0.0)
+    rows = q.shape[0]
     parts = []
     for h in range(2):
-        cols = slice(h * HD, (h + 1) * HD)
-        qh = q[:, cols]
-        s0, s1, s2 = [nt_dot(k[:, cols], qh) for k in keys]
-        scores = jnp.where(in_first, s0, jnp.where(in_last, s2, s1)) * scale
-        scores = jnp.where(owned, scores, NEG)
-        top = jnp.max(scores, axis=0, keepdims=True)
-        weights = jnp.where(owned, jnp.exp2(scores - top), 0.0)
-        total = jnp.sum(weights, axis=0, keepdims=True)
-        some = total > 0.0
-        safe = jnp.where(some, total, 1.0)
-        low = weights.astype(jnp.bfloat16)
-        o0, o1, o2 = [tn_dot(v[:, cols], low) for v in vals]
-        summed = jnp.where(in_first, o0, jnp.where(in_last, o2, o1)) / safe
-        parts.append((summed, jnp.where(some, top + jnp.log2(safe), NEG)))
+        lanes = slice(h * rows, (h + 1) * rows)
+        o0, o1, o2 = [nn_dot(vt[h * HD : (h + 1) * HD], low[:, lanes]) for vt in vts]
+        summed = jnp.where(in_first[:, lanes], o0, jnp.where(in_last[:, lanes], o2, o1))
+        parts.append((summed * inverse[:, lanes], lse[:, lanes]))
     return pack_piece(parts)
 
 
@@ -215,9 +233,9 @@
 
 
 def layer_kernel(
-    q, k, v, cq, ids, db_hbm, w_hbm, out,
-    db, w, kv0, qin, cqin, sp, stx, cp, ctx, att, ptx, prx, ids_tx, ids_rx, ids_s,
-    db_sem, w_sem, ids_sem, kv_ss, kv_rs, q_ss, q_rs, cq_ss, cq_rs, sp_ss, sp_rs, cp_ss, cp_rs,
+    q_hbm, k_hbm, v_hbm, cq_hbm, ids, db_hbm, w_hbm, out,
+    q, k, v, cq, vt, dvt, db, w, k0, vt0, qin, cqin, sp, stx, cp, ctx, att, ptx, prx, ids_tx, ids_rx, ids_s,
+    in_sem, db_sem, w_sem, ids_sem, kv_ss, kv_rs, q_ss, q_rs, cq_ss, cq_rs, sp_ss, sp_rs, cp_ss, cp_rs,
     i1_ss, i1_rs, i2_ss, i2_rs, p_ss, p_rs,
 ):
     d = lax.axis_index("dp")
@@ -239,6 +257,12 @@
             src_ref=src, dst_ref=dst, send_sem=ss, recv_sem=rs, device_id=where, device_id_type=MESH
         )
 
+    in_copies = [
+        pltpu.make_async_copy(src, dst, in_sem.at[i])
+        for i, (src, dst) in enumerate(((v_hbm, v), (cq_hbm, cq), (q_hbm, q), (k_hbm, k)))
+    ]
+    for copy in in_copies:
+        copy.start()
     db_copy = pltpu.make_async_copy(db_hbm, db, db_sem)
     db_copy.start()
     w_copies = [
@@ -254,24 +278,35 @@
     for j in range(1, 4):
         pl.semaphore_signal(barrier, inc=1, device_id={"seq": lax.rem(s + j, 4)}, device_id_type=MESH)
     pl.semaphore_signal(barrier, inc=1, device_id={"mp": other}, device_id_type=MESH)
+
+    def turned(block):
+        return jnp.concatenate([block[:, :HD].T, block[:, HD:].T], axis=0)
+
+    in_copies[0].wait()
+
+    @pl.loop(0, chunks)
+    def _(c):
+        vt[c] = turned(v[:, cols_of(c)])
+
     pl.semaphore_wait(barrier, dps + 3)
 
     def id_hop():
         return remote(ids, ids_tx.at[1], i1_ss, i1_rs, seq=lax.rem(s + 1, 4))
 
     def kv_hop(c, which):
-        return remote((k, v)[which].at[:, cols_of(c)], kv0.at[c, which], kv_ss.at[c, which], kv_rs.at[c, which], seq=1)
+        src, dst = ((k_hbm.at[:, cols_of(c)], k0), (vt.at[c], vt0))[which]
+        return remote(src, dst.at[c], kv_ss.at[c, which], kv_rs.at[c, which], seq=1)
 
     def q_hop(c, dest):
         slot = jnp.maximum(s - 2, 0)
-        return remote(q.at[:, cols_of(c)], qin.at[slot, c], q_ss.at[dest - 1, c], q_rs.at[slot, c], seq=dest)
+        return remote(q_hbm.at[:, cols_of(c)], qin.at[slot, c], q_ss.at[dest - 1, c], q_rs.at[slot, c], seq=dest)
 
     def q_arrived(c, slot):
-        remote(q.at[:, cols_of(c)], qin.at[slot, c], q_ss.at[0, c], q_rs.at[slot, c], seq=1).wait_recv()
+        remote(q_hbm.at[:, cols_of(c)], qin.at[slot, c], q_ss.at[0, c], q_rs.at[slot, c], seq=1).wait_recv()
 
     def cq_hop(c, j):
         return remote(
-            cq.at[:, cols_of(c)], cqin.at[j, c], cq_ss.at[j, c], cq_rs.at[j, c], dp=lax.rem(d + j, dps)
+            cq_hbm.at[:, cols_of(c)], cqin.at[j, c], cq_ss.at[j, c], cq_rs.at[j, c], dp=lax.rem(d + j, dps)
         )
 
     def sp_hop(c, slot, dest, place):
@@ -311,8 +346,6 @@
         def _(j):
             cq_hop(c, j).start()
 
-        cqin[0, c] = cq[:, cols_of(c)]
-
     for copy in w_copies:
         copy.start()
 
@@ -333,14 +366,16 @@
     neutral = jnp.concatenate(
         [jnp.zeros((PAIR, HD), jnp.bfloat16), jnp.full((16, HD), NEG, jnp.bfloat16)], axis=0
     )
-    key_at = lax.broadcasted_iota(jnp.int32, (rows, HD), 0)
-    query_at = lax.broadcasted_iota(jnp.int32, (rows, HD), 1)
+    key_at = lax.broadcasted_iota(jnp.int32, (rows, 2 * rows), 0)
+    query_at = lax.rem(lax.broadcasted_iota(jnp.int32, (rows, 2 * rows), 1), rows)
     causal = key_at <= query_at
+    for copy in in_copies[1:]:
+        copy.wait()
 
     @pl.loop(0, chunks)
     def _(c):
         cols = cols_of(c)
-        sp[0, c] = attend_pair(q[:, cols], k[:, cols], v[:, cols], scale, causal)
+        sp[0, c] = attend_pair(q[:, cols], k[:, cols], vt[c], scale, causal)
 
         @pl.when(s < 1)
         def _():
@@ -357,7 +392,7 @@
     ids_copy.wait()
     db_copy.wait()
 
-    lane = lax.broadcasted_iota(jnp.int32, (1, HD), 1)
+    lane = lax.rem(lax.broadcasted_iota(jnp.int32, (1, 2 * rows), 1), rows)
     in_first = lane < SPAN - 1
     in_last = lane == 2 * SPAN - 1
     live = jnp.logical_or(lane >= SPAN - 1, s > 0)
@@ -370,49 +405,53 @@
         def _():
             kv_hop(c, 0).wait_recv()
             kv_hop(c, 1).wait_recv()
-            k0 = kv0[c, 0]
-            v0 = kv0[c, 1]
-            sp[1, c] = attend_pair(q[:, cols], k0, v0, scale)
+            sp[1, c] = attend_pair(q[:, cols], k0[c], vt0[c], scale)
 
             @pl.loop(0, 2)
             def _(slot):
                 q_arrived(c, slot)
-                both_k = jnp.concatenate([kv0[c, 0], k[:, cols]], axis=0)
-                both_v = jnp.concatenate([kv0[c, 1], v[:, cols]], axis=0)
+                both_k = jnp.concatenate([k0[c], k[:, cols]], axis=0)
+                both_v = jnp.concatenate([vt0[c], vt[c]], axis=1)
                 stx[slot, c] = attend_pair(qin[slot, c], both_k, both_v, scale)
                 sp_hop(c, slot, 2 + slot, 1).start()
 
         @pl.when(s == 2)
         def _():
             q_arrived(c, 1)
-            stx[1, c] = attend_pair(qin[1, c], k[:, cols], v[:, cols], scale)
+            stx[1, c] = attend_pair(qin[1, c], k[:, cols], vt[c], scale)
             sp_hop(c, 1, 3, 2).start()
 
-        @pl.loop(0, dps)
-        def _(turn):
-            j = lax.rem(turn + 1, dps)
-
-            @pl.when(j > 0)
-            def _():
-                cq_hop(c, j).wait_recv()
-
-            keys, vals, shards = [], [], []
+        @pl.loop(0, db.shape[1])
+        def _(b):
+            dvt[b] = turned(db[1, b, :, cols])
+
+        def cross_part(j):
+            keys, vts, shards = [], [], []
             for which, span in ((1, 1), (0, 0), (0, 1)):
                 blocks = [ids_s[j, which, 0, span * 4 + n * 2 + 1] for n in range(NEIGH)]
                 shards.append([ids_s[j, which, 0, span * 4 + n * 2] for n in range(NEIGH)])
                 keys.append(jnp.concatenate([db[0, b, :, cols] for b in blocks], axis=0))
-                vals.append(jnp.concatenate([db[1, b, :, cols] for b in blocks], axis=0))
+                vts.append(jnp.concatenate([dvt[b] for b in blocks], axis=1))
             owned = []
             for n in range(NEIGH):
                 shard = jnp.where(in_first, shards[0][n], jnp.where(in_last, shards[2][n], shards[1][n]))
                 row = jnp.where(jnp.logical_and(shard == d, live), 1, 0)
-                owned.append(jnp.broadcast_to(row, (RETR, HD)))
+                owned.append(jnp.broadcast_to(row, (RETR, 2 * rows)))
             owned = jnp.concatenate(owned, axis=0) > 0
-            ctx[j, c] = cross_pair(cqin[j, c], keys, vals, owned, in_first, in_last, scale)
-
-            @pl.when(j > 0)
-            def _():
-                cp_hop(c, j).start()
+            asked = cq[:, cols] if j == 0 else cqin[j, c]
+            return cross_pair(asked, keys, vts, owned, in_first, in_last, scale)
+
+        for group in range(1, dps + 1, 2):
+            turns = [turn % dps for turn in range(group, min(group + 2, dps + 1))]
+            for j in turns:
+                if j > 0:
+                    cq_hop(c, j).wait_recv()
+            found = [cross_part(j) for j in turns]
+            for j, piece in zip(turns, found):
+                ctx[j, c] = piece
+            for j in turns:
+                if j > 0:
+                    cp_hop(c, j).start()
 
     @pl.loop(0, chunks)
     def _(c):
@@ -507,9 +546,16 @@
     vmem = pl.BlockSpec(memory_space=pltpu.VMEM)
     anywhere = pl.BlockSpec(memory_space=pl.ANY)
     scratch = [
+        pltpu.VMEM((rows, feat), bf16),
+        pltpu.VMEM((rows, feat), bf16),
+        pltpu.VMEM((rows, feat), bf16),
+        pltpu.VMEM((rows, feat), bf16),
+        pltpu.VMEM((chunks, PAIR, rows), bf16),
+        pltpu.VMEM((database.shape[2], PAIR, RETR), bf16),
         pltpu.VMEM(database.shape[1:], bf16),
         pltpu.VMEM((2, feat, half), bf16),
-        pltpu.VMEM((chunks, 2, rows, PAIR), bf16),
+        pltpu.VMEM((chunks, rows, PAIR), bf16),
+        pltpu.VMEM((chunks, PAIR, rows), bf16),
         pltpu.VMEM((2, chunks, rows, PAIR), bf16),
         pltpu.VMEM((dps, chunks, rows, PAIR), bf16),
         pltpu.VMEM((3, chunks, PIECE, rows), bf16),
@@ -522,7 +568,7 @@
         pltpu.VMEM((2, 8, 128), jnp.int32),
         pltpu.VMEM((dps, 2, 8, 128), jnp.int32),
         pltpu.SMEM((dps, 2, 8, 128), jnp.int32),
-        dma, dma((2,)), dma,
+        dma((4,)), dma, dma((2,)), dma,
         dma((chunks, 2)), dma((chunks, 2)),
         dma((2, chunks)), dma((2, chunks)),
         dma((dps, chunks)), dma((dps, chunks)),
@@ -535,11 +581,11 @@
     result = pl.pallas_call(
         layer_kernel,
         out_shape=jax.ShapeDtypeStruct((rows, half), bf16),
-        in_specs=[vmem] * 5 + [anywhere] * 2,
+        in_specs=[anywhere] * 4 + [vmem] + [anywhere] * 2,
         out_specs=vmem,
         scratch_shapes=scratch,
         compiler_params=pltpu.CompilerParams(
-            collective_id=0, has_side_effects=True, vmem_limit_bytes=50 * 1024 * 1024
+            collective_id=0, has_side_effects=True, vmem_limit_bytes=60 * 1024 * 1024
         ),
         cost_estimate=pl.CostEstimate(
             flops=flops, bytes_accessed=2 * (feat * width + database.size), transcendentals=0

time: 59.5 us -> 56.5 us (0.950)
  local copies, waits for them, and re-layouts: 5.36 us -> 3.24 us
  Pallas kernels: 53.9 us -> 53.1 us
    unnamed x9 -> x1, local copies, waits for them, and re-layouts: 4.6 us -> 1.88 us
    pallas_call x1, Pallas kernels: 53.9 us -> 53.1 us  [fused_device(): pl.pallas_call(layer_kernel, out_shape=jax.ShapeDtypeStruct((rows, half),...]
where the time goes in v2:
time: 56.5 us; the launch traced here: 56.3 us
  Pallas kernels  53.1 us (94%)
  local copies, waits for them, and re-layouts  3.24 us (6%)
    pallas_call x1, Pallas kernels, fused_device(): pl.pallas_call(layer_kernel, out_shape=jax.ShapeDtypeStruct((rows, half),...  53.1 us
    unnamed x1, local copies, waits for them, and re-layouts  1.88 us

profile of v2, /device:TPU:8, one launch (start us, length us, event | category | flops | bytes accessed | tf_op | source)
XLA Modules:
  0.0 56.3 jit_solution(18171234197376912504)
XLA Ops:
  0.0 0.8 %reshape.3 = s32[1,8]{1,0:T(1,128)S(1)} reshape(s32[1,2,2,2]{3,2,1,0:T(2,128)} %param.11) | data formatting | bytes 64 | tf_op jit(solution)/shard_map/reshape | solution.py:542
  0.8 0.6 %pad.4.ids = s32[8,128]{1,0:T(8,128)} pad(s32[1,8]{1,0:T(1,128)S(1)} %reshape.3, s32[]{:T(128)} %constant.0.clone.1), padding=0_7x0_120 | pad | bytes 4132 | tf_op jit(solution)/shard_map/jit(_pad)/pad | solution.py:543
  1.4 53.1 %shard_map.73 = bf16[128,2048]{1,0:T(8,128)(2,1)} custom-call(bf16[128,1024]{1,0:T(8,128)(2,1)} %bitcast.8, bf16[128,1024]{1,0:T(8,128)(2,1)} %bitcast.9, bf16[128,1024]{1,0:T(8,128)(2,1)} %bitcast.10, bf16[128,1024]{1,0:T(8,128)(2,1)} %bitcast.11, s32[8,128]{1,0:T(8,128)} %pad.4.ids, bf16[2,6,128,1024]{3,2,1,0:T(8,128)(2,1)} %bitcast.6, ...), custom_call_target="tpu_custom_call" | custom-call | flops 3221225472 | bytes 11534336 | tf_op jit(solution)/shard_map/pallas_call | solution.py:581
  54.5 1.9 %copy.9 = bf16[1,128,2048]{2,1,0:T(8,128)(2,1)} copy(bf16[1,128,2048]{2,1,0:T(8,128)(2,1)} %bitcast.7) | data formatting | bytes 1048576

commit v3 on v2

--- a/solution.py
+++ b/solution.py
@@ -226,10 +226,11 @@
     top = functools.reduce(jnp.maximum, lses)
     shares = [jnp.exp2(lse - top) for lse in lses]
     total = functools.reduce(jnp.add, shares)
+    inverse = 1.0 / total
     summed = 0.0
     for piece, share in zip(pieces, shares):
-        summed = summed + piece[h * HD : (h + 1) * HD, :].astype(jnp.float32) * (share / total)
-    return summed
+        summed = summed + piece[h * HD : (h + 1) * HD, :].astype(jnp.float32) * (share * inverse)
+    return summed, jnp.maximum(top + jnp.log2(total), NEG)
 
 
 def layer_kernel(
@@ -272,9 +273,12 @@
         for i, side in enumerate((other, m))
     ]
 
+    def peer(j):
+        return (d, d + 1 - 2 * lax.rem(d, 2), lax.rem(d + 2, 4), 3 - d)[j]
+
     barrier = pltpu.get_barrier_semaphore()
     for j in range(1, dps):
-        pl.semaphore_signal(barrier, inc=1, device_id={"dp": lax.rem(d + j, dps)}, device_id_type=MESH)
+        pl.semaphore_signal(barrier, inc=1, device_id={"dp": peer(j)}, device_id_type=MESH)
     for j in range(1, 4):
         pl.semaphore_signal(barrier, inc=1, device_id={"seq": lax.rem(s + j, 4)}, device_id_type=MESH)
     pl.semaphore_signal(barrier, inc=1, device_id={"mp": other}, device_id_type=MESH)
@@ -305,20 +309,19 @@
         remote(q_hbm.at[:, cols_of(c)], qin.at[slot, c], q_ss.at[0, c], q_rs.at[slot, c], seq=1).wait_recv()
 
     def cq_hop(c, j):
-        return remote(
-            cq_hbm.at[:, cols_of(c)], cqin.at[j, c], cq_ss.at[j, c], cq_rs.at[j, c], dp=lax.rem(d + j, dps)
-        )
+        src = cqin.at[2, c] if j == 3 else cq_hbm.at[:, cols_of(c)]
+        return remote(src, cqin.at[j, c], cq_ss.at[j, c], cq_rs.at[j, c], dp=peer(1 if j == 3 else j))
 
     def sp_hop(c, slot, dest, place):
         return remote(stx.at[slot, c], sp.at[place, c], sp_ss.at[slot, c], sp_rs.at[place, c], seq=dest)
 
     def cp_hop(c, j):
         return remote(
-            ctx.at[j, c], cp.at[j, c], cp_ss.at[j, c], cp_rs.at[j, c], dp=lax.rem(d - j + dps, dps)
+            ctx.at[j, c], cp.at[j, c], cp_ss.at[j, c], cp_rs.at[j, c], dp=peer(1 if j == 3 else j)
         )
 
     def id_share(j):
-        return remote(ids_tx, ids_rx.at[j], i2_ss.at[j], i2_rs.at[j], dp=lax.rem(d + j, dps))
+        return remote(ids_tx, ids_rx.at[j], i2_ss.at[j], i2_rs.at[j], dp=peer(j))
 
     def p_hop(t):
         return remote(ptx.at[t], prx.at[t], p_ss.at[t], p_rs.at[t], mp=other)
@@ -342,9 +345,8 @@
         def _():
             q_hop(c, 2).start()
 
-        @pl.loop(1, dps)
-        def _(j):
-            cq_hop(c, j).start()
+        cq_hop(c, 2).start()
+        cq_hop(c, 1).start()
 
     for copy in w_copies:
         copy.start()
@@ -400,6 +402,8 @@
     @pl.loop(0, chunks)
     def _(c):
         cols = cols_of(c)
+        cq_hop(c, 2).wait_recv()
+        cq_hop(c, 3).start()
 
         @pl.when(s == 1)
         def _():
@@ -428,8 +432,8 @@
         def cross_part(j):
             keys, vts, shards = [], [], []
             for which, span in ((1, 1), (0, 0), (0, 1)):
-                blocks = [ids_s[j, which, 0, span * 4 + n * 2 + 1] for n in range(NEIGH)]
-                shards.append([ids_s[j, which, 0, span * 4 + n * 2] for n in range(NEIGH)])
+                blocks = [ids_s[j, which, span, n, 1] for n in range(NEIGH)]
+                shards.append([ids_s[j, which, span, n, 0] for n in range(NEIGH)])
                 keys.append(jnp.concatenate([db[0, b, :, cols] for b in blocks], axis=0))
                 vts.append(jnp.concatenate([dvt[b] for b in blocks], axis=1))
             owned = []
@@ -441,17 +445,19 @@
             asked = cq[:, cols] if j == 0 else cqin[j, c]
             return cross_pair(asked, keys, vts, owned, in_first, in_last, scale)
 
-        for group in range(1, dps + 1, 2):
-            turns = [turn % dps for turn in range(group, min(group + 2, dps + 1))]
-            for j in turns:
-                if j > 0:
-                    cq_hop(c, j).wait_recv()
-            found = [cross_part(j) for j in turns]
-            for j, piece in zip(turns, found):
-                ctx[j, c] = piece
-            for j in turns:
-                if j > 0:
-                    cp_hop(c, j).start()
+        cq_hop(c, 3).wait_recv()
+        across, beside = cross_part(2), cross_part(3)
+        ctx[3, c] = beside
+        cp_hop(c, 3).start()
+        cq_hop(c, 1).wait_recv()
+        near, own = cross_part(1), cross_part(0)
+        ctx[1, c] = near
+        ctx[0, c] = own
+        cp_hop(c, 1).start()
+        cp_hop(c, 3).wait_recv()
+        both = [across, cp[3, c]]
+        ctx[2, c] = pack_piece([merge_pieces(both, h) for h in range(2)])
+        cp_hop(c, 2).start()
 
     @pl.loop(0, chunks)
     def _(c):
@@ -463,12 +469,12 @@
         def _():
             sp_hop(c, 0, 3, 2).wait_recv()
 
-        for j in range(1, dps):
-            cp_hop(c, j).wait_recv()
+        cp_hop(c, 1).wait_recv()
+        cp_hop(c, 2).wait_recv()
         self_pieces = [sp[i, c] for i in range(3)]
-        cross_pieces = [ctx[0, c]] + [cp[j, c] for j in range(1, dps)]
+        cross_pieces = [ctx[0, c], cp[1, c], cp[2, c]]
         for h in range(2):
-            both = merge_pieces(self_pieces, h) + merge_pieces(cross_pieces, h)
+            both = merge_pieces(self_pieces, h)[0] + merge_pieces(cross_pieces, h)[0]
             att[:, pl.ds(pl.multiple_of(c * PAIR + h * HD, HD), HD)] = both.T.astype(jnp.bfloat16)
 
     def tile_cols(t):
@@ -522,8 +528,7 @@
         def _():
             sp_hop(c, 1, 3, 2).wait_send()
 
-        @pl.loop(1, dps)
-        def _(j):
+        for j in range(1, dps):
             cq_hop(c, j).wait_send()
             cp_hop(c, j).wait_send()
 
@@ -539,8 +544,7 @@
     width = out_weight.shape[1]
     half = width // 2
     tiles = half // TILE
-    ids = neighbour_ids.reshape(1, -1)
-    ids = jnp.pad(ids, ((0, 7), (0, 128 - ids.shape[1])))
+    ids = neighbour_ids[0]
     bf16 = jnp.bfloat16
     dma = pltpu.SemaphoreType.DMA
     vmem = pl.BlockSpec(memory_space=pltpu.VMEM)
@@ -565,9 +569,9 @@
         pltpu.VMEM((rows, feat), bf16),
         pltpu.VMEM((tiles, rows, TILE), bf16),
         pltpu.VMEM((tiles, rows, TILE), bf16),
-        pltpu.VMEM((2, 8, 128), jnp.int32),
-        pltpu.VMEM((dps, 2, 8, 128), jnp.int32),
-        pltpu.SMEM((dps, 2, 8, 128), jnp.int32),
+        pltpu.VMEM((2,) + ids.shape, jnp.int32),
+        pltpu.VMEM((dps, 2) + ids.shape, jnp.int32),
+        pltpu.SMEM((dps, 2) + ids.shape, jnp.int32),
         dma((4,)), dma, dma((2,)), dma,
         dma((chunks, 2)), dma((chunks, 2)),
         dma((2, chunks)), dma((2, chunks)),
@@ -604,7 +608,7 @@
         P("dp", None, None, None, "mp"),
         P("mp", None),
     )
-    fits = mesh.shape["seq"] == 4 and mesh.shape["mp"] == 2
+    fits = mesh.shape["seq"] == 4 and mesh.shape["mp"] == 2 and mesh.shape["dp"] == 4
     return jax.shard_map(
         fused_device if fits else per_device,
         mesh=mesh,

time: 56.5 us -> 49.5 us (0.88)
  Pallas kernels: 53.1 us -> 47.4 us
  local copies, waits for them, and re-layouts: 3.24 us -> 1.88 us
    pallas_call x1, Pallas kernels: 53.1 us -> 47.4 us  [fused_device(): pl.pallas_call(layer_kernel, out_shape=jax.ShapeDtypeStruct((rows, half),...]
    reshape x1 -> x0, local copies, waits for them, and re-layouts: 0.76 us -> none  [fused_device(): ids = neighbour_ids.reshape(1, -1)]
    pad x1 -> x0, local copies, waits for them, and re-layouts: 0.6 us -> none  [fused_device(): ids = jnp.pad(ids, ((0, 7), (0, 128 - ids.shape[1])))]
where the time goes in v3:
time: 49.5 us; the launch traced here: 49.3 us
  Pallas kernels  47.4 us (96%)
  local copies, waits for them, and re-layouts  1.88 us (4%)
    pallas_call x1, Pallas kernels, fused_device(): pl.pallas_call(layer_kernel, out_shape=jax.ShapeDtypeStruct((rows, half),...  47.4 us
    unnamed x1, local copies, waits for them, and re-layouts  1.88 us

profile of v3, /device:TPU:8, one launch (start us, length us, event | category | flops | bytes accessed | tf_op | source)
XLA Modules:
  0.0 49.3 jit_solution(15416935682069659351)
XLA Ops:
  0.0 47.4 %shard_map.73 = bf16[128,2048]{1,0:T(8,128)(2,1)} custom-call(bf16[128,1024]{1,0:T(8,128)(2,1)} %bitcast.9, bf16[128,1024]{1,0:T(8,128)(2,1)} %bitcast.10, bf16[128,1024]{1,0:T(8,128)(2,1)} %bitcast.11, bf16[128,1024]{1,0:T(8,128)(2,1)} %bitcast.12, s32[2,2,2]{2,1,0:T(2,128)} %bitcast.13, bf16[2,6,128,1024]{3,2,1,0:T(8,128)(2,1)} %bitcast.7, ...), custom_call_target="tpu_custom_call" | custom-call | flops 3221225472 | bytes 11534336 | tf_op jit(solution)/shard_map/pallas_call | solution.py:585
  47.4 1.9 %copy.9 = bf16[1,128,2048]{2,1,0:T(8,128)(2,1)} copy(bf16[1,128,2048]{2,1,0:T(8,128)(2,1)} %bitcast.8) | data formatting | bytes 1048576

commit v4 on v3

--- a/solution.py
+++ b/solution.py
@@ -137,7 +137,7 @@
 NEG = -1e30
 LOG2E = 1.4426950408889634
 PAIR = 2 * HD
-PIECE = PAIR + 16
+PIECE = HD + 16
 TILE = 512
 MESH = pl.DeviceIdType.MESH
 
@@ -150,19 +150,15 @@
     return jnp.dot(a, b, preferred_element_type=jnp.float32)
 
 
-def pack_piece(parts):
-    row = lax.broadcasted_iota(jnp.int32, (16, HD), 0)
-    stats = jnp.zeros((16, HD), jnp.float32)
-    for index, (_, lse) in enumerate(parts):
-        rest = lse
-        for term in range(3):
-            rounded = rest.astype(jnp.bfloat16).astype(jnp.float32)
-            stats = jnp.where(row == 3 * index + term, rounded, stats)
-            rest = rest - rounded
-    return jnp.concatenate(
-        [parts[0][0].astype(jnp.bfloat16), parts[1][0].astype(jnp.bfloat16), stats.astype(jnp.bfloat16)],
-        axis=0,
-    )
+def pack_piece(summed, lse):
+    row = lax.broadcasted_iota(jnp.int32, (16, summed.shape[1]), 0)
+    stats = jnp.zeros(row.shape, jnp.float32)
+    rest = lse
+    for term in range(3):
+        rounded = rest.astype(jnp.bfloat16).astype(jnp.float32)
+        stats = jnp.where(row == term, rounded, stats)
+        rest = rest - rounded
+    return jnp.concatenate([summed.astype(jnp.bfloat16), stats.astype(jnp.bfloat16)], axis=0)
 
 
 def by_head(q):
@@ -183,59 +179,54 @@
     return weights.astype(jnp.bfloat16), top, total
 
 
+def sum_values(vt, low):
+    both = nn_dot(vt, low)
+    lane = lax.broadcasted_iota(jnp.int32, (HD, low.shape[1]), 1)
+    return jnp.where(lane < low.shape[1] // 2, both[:HD], both[HD:])
+
+
 def attend_pair(q, k, vt, scale, allowed=None):
     scores = nt_dot(k, by_head(q))
     if allowed is not None:
         scores = jnp.where(allowed, scores, NEG)
     low, top, total = weigh(scores, scale)
-    lse = top * scale + jnp.log2(total)
-    inverse = 1.0 / total
-    rows = q.shape[0]
-    parts = []
-    for h in range(2):
-        lanes = slice(h * rows, (h + 1) * rows)
-        summed = nn_dot(vt[h * HD : (h + 1) * HD], low[:, lanes]) * inverse[:, lanes]
-        parts.append((summed, lse[:, lanes]))
-    return pack_piece(parts)
-
-
-def cross_pair(q, keys, vts, owned, in_first, in_last, scale):
+    return pack_piece(sum_values(vt, low) * (1.0 / total), top * scale + jnp.log2(total))
+
+
+def cross_pair(q, keys, vts, owned, first, scale):
     both = by_head(q)
-    s0, s1, s2 = [nt_dot(k, both) for k in keys]
-    scores = jnp.where(in_first, s0, jnp.where(in_last, s2, s1))
+    scores = nt_dot(keys[0], both)
+    if len(keys) > 1:
+        scores = jnp.where(first, scores, nt_dot(keys[1], both))
     scores = jnp.where(owned, scores, NEG)
     low, top, total = weigh(scores, scale)
     some = top > 0.5 * NEG
     lse = jnp.where(some, top * scale + jnp.log2(total), NEG)
     inverse = jnp.where(some, 1.0 / total, 0.0)
-    rows = q.shape[0]
-    parts = []
-    for h in range(2):
-        lanes = slice(h * rows, (h + 1) * rows)
-        o0, o1, o2 = [nn_dot(vt[h * HD : (h + 1) * HD], low[:, lanes]) for vt in vts]
-        summed = jnp.where(in_first[:, lanes], o0, jnp.where(in_last[:, lanes], o2, o1))
-        parts.append((summed * inverse[:, lanes], lse[:, lanes]))
-    return pack_piece(parts)
-
-
-def merge_pieces(pieces, h):
+    summed = sum_values(vts[0], low)
+    if len(keys) > 1:
+        summed = jnp.where(first, summed, sum_values(vts[1], low))
+    return pack_piece(summed * inverse, lse)
+
+
+def merge_pieces(pieces):
     lses = []
     for piece in pieces:
-        stats = piece[PAIR:, :].astype(jnp.float32)
-        lses.append(stats[3 * h : 3 * h + 1] + stats[3 * h + 1 : 3 * h + 2] + stats[3 * h + 2 : 3 * h + 3])
+        stats = piece[HD:, :].astype(jnp.float32)
+        lses.append(stats[0:1] + stats[1:2] + stats[2:3])
     top = functools.reduce(jnp.maximum, lses)
     shares = [jnp.exp2(lse - top) for lse in lses]
     total = functools.reduce(jnp.add, shares)
     inverse = 1.0 / total
     summed = 0.0
     for piece, share in zip(pieces, shares):
-        summed = summed + piece[h * HD : (h + 1) * HD, :].astype(jnp.float32) * (share * inverse)
+        summed = summed + piece[:HD, :].astype(jnp.float32) * (share * inverse)
     return summed, jnp.maximum(top + jnp.log2(total), NEG)
 
 
 def layer_kernel(
     q_hbm, k_hbm, v_hbm, cq_hbm, ids, db_hbm, w_hbm, out,
-    q, k, v, cq, vt, dvt, db, w, k0, vt0, qin, cqin, sp, stx, cp, ctx, att, ptx, prx, ids_tx, ids_rx, ids_s,
+    q, k, v, cq, qh, cqh, vt, dvt, db, w, k0, vt0, qin, cqin, sp, stx, cp, ctx, att, ptx, prx, ids_tx, ids_rx, ids_s,
     in_sem, db_sem, w_sem, ids_sem, kv_ss, kv_rs, q_ss, q_rs, cq_ss, cq_rs, sp_ss, sp_rs, cp_ss, cp_rs,
     i1_ss, i1_rs, i2_ss, i2_rs, p_ss, p_rs,
 ):
@@ -243,8 +234,11 @@
     s = lax.axis_index("seq")
     m = lax.axis_index("mp")
     dps = cqin.shape[0]
-    chunks = cqin.shape[1]
+    steps = cqin.shape[1]
+    chunks = steps // 2
     rows = q.shape[0]
+    few = rows // 2
+    turn = SPAN - 1
     half = out.shape[1]
     tiles = half // TILE
     scale = LOG2E / math.sqrt(HD)
@@ -260,7 +254,7 @@
 
     in_copies = [
         pltpu.make_async_copy(src, dst, in_sem.at[i])
-        for i, (src, dst) in enumerate(((v_hbm, v), (cq_hbm, cq), (q_hbm, q), (k_hbm, k)))
+        for i, (src, dst) in enumerate(((cq_hbm, cq), (q_hbm, q), (v_hbm, v), (k_hbm, k)))
     ]
     for copy in in_copies:
         copy.start()
@@ -286,10 +280,16 @@
     def turned(block):
         return jnp.concatenate([block[:, :HD].T, block[:, HD:].T], axis=0)
 
-    in_copies[0].wait()
+    for copy in in_copies[:3]:
+        copy.wait()
 
     @pl.loop(0, chunks)
     def _(c):
+        for src, dst in ((cq, cqh), (q, qh)):
+            moved = pltpu.roll(src[:, cols_of(c)].astype(jnp.float32), rows - turn, axis=0)
+            moved = moved.astype(jnp.bfloat16)
+            dst[c] = moved[:few]
+            dst[chunks + c] = moved[few:]
         vt[c] = turned(v[:, cols_of(c)])
 
     pl.semaphore_wait(barrier, dps + 3)
@@ -303,13 +303,13 @@
 
     def q_hop(c, dest):
         slot = jnp.maximum(s - 2, 0)
-        return remote(q_hbm.at[:, cols_of(c)], qin.at[slot, c], q_ss.at[dest - 1, c], q_rs.at[slot, c], seq=dest)
+        return remote(qh.at[c], qin.at[slot, c], q_ss.at[dest - 1, c], q_rs.at[slot, c], seq=dest)
 
     def q_arrived(c, slot):
-        remote(q_hbm.at[:, cols_of(c)], qin.at[slot, c], q_ss.at[0, c], q_rs.at[slot, c], seq=1).wait_recv()
+        remote(qh.at[c], qin.at[slot, c], q_ss.at[0, c], q_rs.at[slot, c], seq=1).wait_recv()
 
     def cq_hop(c, j):
-        src = cqin.at[2, c] if j == 3 else cq_hbm.at[:, cols_of(c)]
+        src = cqin.at[2, c] if j == 3 else cqh.at[c]
         return remote(src, cqin.at[j, c], cq_ss.at[j, c], cq_rs.at[j, c], dp=peer(1 if j == 3 else j))
 
     def sp_hop(c, slot, dest, place):
@@ -323,30 +323,30 @@
     def id_share(j):
         return remote(ids_tx, ids_rx.at[j], i2_ss.at[j], i2_rs.at[j], dp=peer(j))
 
-    def p_hop(t):
-        return remote(ptx.at[t], prx.at[t], p_ss.at[t], p_rs.at[t], mp=other)
+    def p_hop(r, t):
+        return remote(ptx.at[r, t], prx.at[r, t], p_ss.at[r, t], p_rs.at[r, t], mp=other)
 
     @pl.when(s < 3)
     def _():
         id_hop().start()
 
-    @pl.loop(0, chunks)
-    def _(c):
-        @pl.when(s == 0)
-        def _():
-            kv_hop(c, 0).start()
-            kv_hop(c, 1).start()
+    @pl.loop(0, steps)
+    def _(t):
+        @pl.when(jnp.logical_and(s == 0, t < chunks))
+        def _():
+            kv_hop(t, 0).start()
+            kv_hop(t, 1).start()
 
         @pl.when(s >= 2)
         def _():
-            q_hop(c, 1).start()
+            q_hop(t, 1).start()
 
         @pl.when(s == 3)
         def _():
-            q_hop(c, 2).start()
-
-        cq_hop(c, 2).start()
-        cq_hop(c, 1).start()
+            q_hop(t, 2).start()
+
+        cq_hop(t, 2).start()
+        cq_hop(t, 1).start()
 
     for copy in w_copies:
         copy.start()
@@ -366,26 +366,27 @@
     ids_rx[0] = ids_tx[...]
 
     neutral = jnp.concatenate(
-        [jnp.zeros((PAIR, HD), jnp.bfloat16), jnp.full((16, HD), NEG, jnp.bfloat16)], axis=0
-    )
-    key_at = lax.broadcasted_iota(jnp.int32, (rows, 2 * rows), 0)
-    query_at = lax.rem(lax.broadcasted_iota(jnp.int32, (rows, 2 * rows), 1), rows)
-    causal = key_at <= query_at
-    for copy in in_copies[1:]:
-        copy.wait()
-
-    @pl.loop(0, chunks)
-    def _(c):
-        cols = cols_of(c)
-        sp[0, c] = attend_pair(q[:, cols], k[:, cols], vt[c], scale, causal)
-
-        @pl.when(s < 1)
-        def _():
-            sp[1, c] = neutral
-
-        @pl.when(s < 3)
-        def _():
-            sp[2, c] = neutral
+        [jnp.zeros((HD, rows), jnp.bfloat16), jnp.full((16, rows), NEG, jnp.bfloat16)], axis=0
+    )
+    key_at = lax.broadcasted_iota(jnp.int32, (rows, rows), 0)
+    lane_at = lax.rem(lax.broadcasted_iota(jnp.int32, (rows, rows), 1), few) + turn
+    in_copies[3].wait()
+
+    for r in range(2):
+        causal = key_at <= lax.rem(lane_at + r * few, rows)
+
+        @pl.loop(0, chunks)
+        def _(c):
+            t = r * chunks + c
+            sp[0, t] = attend_pair(qh[t], k[:, cols_of(c)], vt[c], scale, causal)
+
+            @pl.when(s < 1)
+            def _():
+                sp[1, t] = neutral
+
+            @pl.when(s < 3)
+            def _():
+                sp[2, t] = neutral
 
     for j in range(1, dps):
         id_share(j).wait_recv()
@@ -394,108 +395,144 @@
     ids_copy.wait()
     db_copy.wait()
 
-    lane = lax.rem(lax.broadcasted_iota(jnp.int32, (1, 2 * rows), 1), rows)
-    in_first = lane < SPAN - 1
-    in_last = lane == 2 * SPAN - 1
-    live = jnp.logical_or(lane >= SPAN - 1, s > 0)
-
-    @pl.loop(0, chunks)
-    def _(c):
-        cols = cols_of(c)
-        cq_hop(c, 2).wait_recv()
-        cq_hop(c, 3).start()
-
-        @pl.when(s == 1)
-        def _():
-            kv_hop(c, 0).wait_recv()
-            kv_hop(c, 1).wait_recv()
-            sp[1, c] = attend_pair(q[:, cols], k0[c], vt0[c], scale)
-
-            @pl.loop(0, 2)
-            def _(slot):
-                q_arrived(c, slot)
-                both_k = jnp.concatenate([k0[c], k[:, cols]], axis=0)
-                both_v = jnp.concatenate([vt0[c], vt[c]], axis=1)
-                stx[slot, c] = attend_pair(qin[slot, c], both_k, both_v, scale)
-                sp_hop(c, slot, 2 + slot, 1).start()
-
-        @pl.when(s == 2)
-        def _():
-            q_arrived(c, 1)
-            stx[1, c] = attend_pair(qin[1, c], k[:, cols], vt[c], scale)
-            sp_hop(c, 1, 3, 2).start()
-
-        @pl.loop(0, db.shape[1])
-        def _(b):
-            dvt[b] = turned(db[1, b, :, cols])
-
-        def cross_part(j):
-            keys, vts, shards = [], [], []
-            for which, span in ((1, 1), (0, 0), (0, 1)):
-                blocks = [ids_s[j, which, span, n, 1] for n in range(NEIGH)]
-                shards.append([ids_s[j, which, span, n, 0] for n in range(NEIGH)])
-                keys.append(jnp.concatenate([db[0, b, :, cols] for b in blocks], axis=0))
-                vts.append(jnp.concatenate([dvt[b] for b in blocks], axis=1))
-            owned = []
-            for n in range(NEIGH):
-                shard = jnp.where(in_first, shards[0][n], jnp.where(in_last, shards[2][n], shards[1][n]))
-                row = jnp.where(jnp.logical_and(shard == d, live), 1, 0)
-                owned.append(jnp.broadcast_to(row, (RETR, 2 * rows)))
-            owned = jnp.concatenate(owned, axis=0) > 0
-            asked = cq[:, cols] if j == 0 else cqin[j, c]
-            return cross_pair(asked, keys, vts, owned, in_first, in_last, scale)
-
-        cq_hop(c, 3).wait_recv()
-        across, beside = cross_part(2), cross_part(3)
-        ctx[3, c] = beside
-        cp_hop(c, 3).start()
-        cq_hop(c, 1).wait_recv()
-        near, own = cross_part(1), cross_part(0)
-        ctx[1, c] = near
-        ctx[0, c] = own
-        cp_hop(c, 1).start()
-        cp_hop(c, 3).wait_recv()
-        both = [across, cp[3, c]]
-        ctx[2, c] = pack_piece([merge_pieces(both, h) for h in range(2)])
-        cp_hop(c, 2).start()
-
-    @pl.loop(0, chunks)
-    def _(c):
-        @pl.when(s >= 2)
-        def _():
-            sp_hop(c, 0, 2, 1).wait_recv()
-
-        @pl.when(s == 3)
-        def _():
-            sp_hop(c, 0, 3, 2).wait_recv()
-
-        cp_hop(c, 1).wait_recv()
-        cp_hop(c, 2).wait_recv()
-        self_pieces = [sp[i, c] for i in range(3)]
-        cross_pieces = [ctx[0, c], cp[1, c], cp[2, c]]
-        for h in range(2):
-            both = merge_pieces(self_pieces, h)[0] + merge_pieces(cross_pieces, h)[0]
-            att[:, pl.ds(pl.multiple_of(c * PAIR + h * HD, HD), HD)] = both.T.astype(jnp.bfloat16)
+    at_start = lax.rem(lax.broadcasted_iota(jnp.int32, (1, rows), 1), few) == 0
 
     def tile_cols(t):
         return pl.ds(pl.multiple_of(t * TILE, TILE), TILE)
 
-    w_copies[0].wait()
+    def send_merged(t):
+        cp_hop(t, 3).wait_recv()
+        ctx[2, t] = pack_piece(*merge_pieces([ctx[2, t], cp[3, t]]))
+        cp_hop(t, 2).start()
+
+    def forward(t):
+        cq_hop(t, 2).wait_recv()
+        cq_hop(t, 3).start()
+
+    def finish(r):
+        @pl.loop(0, chunks)
+        def _(c):
+            t = r * chunks + c
+
+            @pl.when(s >= 2)
+            def _():
+                sp_hop(t, 0, 2, 1).wait_recv()
+
+            @pl.when(s == 3)
+            def _():
+                sp_hop(t, 0, 3, 2).wait_recv()
+
+            cp_hop(t, 1).wait_recv()
+            cp_hop(t, 2).wait_recv()
+            both = (
+                merge_pieces([sp[i, t] for i in range(3)])[0]
+                + merge_pieces([ctx[0, t], cp[1, t], cp[2, t]])[0]
+            )
+            both = both.T.astype(jnp.bfloat16)
+            for h in range(2):
+                cols = pl.ds(pl.multiple_of(c * PAIR + h * HD, HD), HD)
+                att[r * few : (r + 1) * few, cols] = both[h * few : (h + 1) * few]
+
+        if r == 0:
+            w_copies[0].wait()
+
+        @pl.loop(0, tiles)
+        def _(t):
+            ptx[r, t] = nn_dot(att[r * few : (r + 1) * few, :], w[0, :, tile_cols(t)]).astype(jnp.bfloat16)
+            p_hop(r, t).start()
+
+    def cross_part(r, c, t, j):
+        spans = ((0, 0),) if r == 0 else ((0, 1), (1, 1))
+        keys, vts, shards = [], [], []
+        for which, span in spans:
+            blocks = [ids_s[j, which, span, n, 1] for n in range(NEIGH)]
+            shards.append([ids_s[j, which, span, n, 0] for n in range(NEIGH)])
+            keys.append(jnp.concatenate([db[0, b, :, cols_of(c)] for b in blocks], axis=0))
+            vts.append(jnp.concatenate([dvt[c, b] for b in blocks], axis=1))
+        owned = []
+        for n in range(NEIGH):
+            if r == 0:
+                row = jnp.where(jnp.broadcast_to(shards[0][n], (1, rows)) == d, 1, 0)
+            else:
+                here = jnp.where(at_start, shards[0][n], shards[1][n]) == d
+                row = jnp.where(jnp.logical_and(here, jnp.logical_or(at_start, s > 0)), 1, 0)
+            owned.append(jnp.broadcast_to(row, (RETR, rows)))
+        owned = jnp.concatenate(owned, axis=0) > 0
+        asked = cqh[t] if j == 0 else cqin[j, t]
+        return cross_pair(asked, keys, vts, owned, at_start, scale)
+
+    forward(0)
+
+    for r in range(2):
+
+        @pl.loop(0, chunks)
+        def _(c):
+            t = r * chunks + c
+            cols = cols_of(c)
+
+            if r == 0:
+
+                @pl.loop(0, db.shape[1])
+                def _(b):
+                    dvt[c, b] = turned(db[1, b, :, cols])
+
+            @pl.when(t + 1 < steps)
+            def _():
+                forward(t + 1)
+
+            @pl.when(s == 1)
+            def _():
+                if r == 0:
+                    kv_hop(c, 0).wait_recv()
+                    kv_hop(c, 1).wait_recv()
+                sp[1, t] = attend_pair(qh[t], k0[c], vt0[c], scale)
+
+                @pl.loop(0, 2)
+                def _(slot):
+                    q_arrived(t, slot)
+                    both_k = jnp.concatenate([k0[c], k[:, cols]], axis=0)
+                    both_v = jnp.concatenate([vt0[c], vt[c]], axis=1)
+                    stx[slot, t] = attend_pair(qin[slot, t], both_k, both_v, scale)
+                    sp_hop(t, slot, 2 + slot, 1).start()
+
+            @pl.when(s == 2)
+            def _():
+                q_arrived(t, 1)
+                stx[1, t] = attend_pair(qin[1, t], k[:, cols], vt[c], scale)
+                sp_hop(t, 1, 3, 2).start()
+
+            cq_hop(t, 3).wait_recv()
+            across, beside = cross_part(r, c, t, 2), cross_part(r, c, t, 3)
+            ctx[2, t] = across
+            ctx[3, t] = beside
+            cp_hop(t, 3).start()
+            cq_hop(t, 1).wait_recv()
+            near, own = cross_part(r, c, t, 1), cross_part(r, c, t, 0)
+            ctx[1, t] = near
+            ctx[0, t] = own
+            cp_hop(t, 1).start()
+
+            @pl.when(t > 0)
+            def _():
+                send_merged(t - 1)
+
+            if r == 1:
+
+                @pl.when(c == chunks // 2 - 1)
+                def _():
+                    finish(0)
+
+    send_merged(steps - 1)
+    finish(1)
+    w_copies[1].wait()
 
     @pl.loop(0, tiles)
     def _(t):
-        ptx[t] = jnp.dot(
-            att[...], w[0, :, tile_cols(t)], preferred_element_type=jnp.float32
-        ).astype(jnp.bfloat16)
-        p_hop(t).start()
-
-    w_copies[1].wait()
-
-    @pl.loop(0, tiles)
-    def _(t):
-        own = jnp.dot(att[...], w[1, :, tile_cols(t)], preferred_element_type=jnp.float32)
-        p_hop(t).wait_recv()
-        out[:, tile_cols(t)] = (own + prx[t].astype(jnp.float32)).astype(jnp.bfloat16)
+        own = nn_dot(att[...], w[1, :, tile_cols(t)])
+        p_hop(0, t).wait_recv()
+        p_hop(1, t).wait_recv()
+        other_part = jnp.concatenate([prx[0, t], prx[1, t]], axis=0).astype(jnp.float32)
+        out[:, tile_cols(t)] = pltpu.roll(own + other_part, turn, axis=0).astype(jnp.bfloat16)
 
     @pl.when(s < 3)
     def _():
@@ -504,9 +541,9 @@
     for j in range(1, dps):
         id_share(j).wait_send()
 
-    @pl.loop(0, chunks)
+    @pl.loop(0, steps)
     def _(c):
-        @pl.when(s == 0)
+        @pl.when(jnp.logical_and(s == 0, c < chunks))
         def _():
             kv_hop(c, 0).wait_send()
             kv_hop(c, 1).wait_send()
@@ -534,13 +571,16 @@
 
     @pl.loop(0, tiles)
     def _(t):
-        p_hop(t).wait_send()
+        p_hop(0, t).wait_send()
+        p_hop(1, t).wait_send()
 
 
 def fused_device(queries, keys, values, cross_queries, neighbour_ids, database, out_weight):
     rows, feat = queries.shape[1:]
     dps = lax.axis_size("dp")
     chunks = feat // PAIR
+    steps = 2 * chunks
+    few = rows // 2
     width = out_weight.shape[1]
     half = width // 2
     tiles = half // TILE
@@ -554,32 +594,34 @@
         pltpu.VMEM((rows, feat), bf16),
         pltpu.VMEM((rows, feat), bf16),
         pltpu.VMEM((rows, feat), bf16),
+        pltpu.VMEM((steps, few, PAIR), bf16),
+        pltpu.VMEM((steps, few, PAIR), bf16),
         pltpu.VMEM((chunks, PAIR, rows), bf16),
-        pltpu.VMEM((database.shape[2], PAIR, RETR), bf16),
+        pltpu.VMEM((chunks, database.shape[2], PAIR, RETR), bf16),
         pltpu.VMEM(database.shape[1:], bf16),
         pltpu.VMEM((2, feat, half), bf16),
         pltpu.VMEM((chunks, rows, PAIR), bf16),
         pltpu.VMEM((chunks, PAIR, rows), bf16),
-        pltpu.VMEM((2, chunks, rows, PAIR), bf16),
-        pltpu.VMEM((dps, chunks, rows, PAIR), bf16),
-        pltpu.VMEM((3, chunks, PIECE, rows), bf16),
-        pltpu.VMEM((2, chunks, PIECE, rows), bf16),
-        pltpu.VMEM((dps, chunks, PIECE, rows), bf16),
-        pltpu.VMEM((dps, chunks, PIECE, rows), bf16),
+        pltpu.VMEM((2, steps, few, PAIR), bf16),
+        pltpu.VMEM((dps, steps, few, PAIR), bf16),
+        pltpu.VMEM((3, steps, PIECE, rows), bf16),
+        pltpu.VMEM((2, steps, PIECE, rows), bf16),
+        pltpu.VMEM((dps, steps, PIECE, rows), bf16),
+        pltpu.VMEM((dps, steps, PIECE, rows), bf16),
         pltpu.VMEM((rows, feat), bf16),
-        pltpu.VMEM((tiles, rows, TILE), bf16),
-        pltpu.VMEM((tiles, rows, TILE), bf16),
+        pltpu.VMEM((2, tiles, few, TILE), bf16),
+        pltpu.VMEM((2, tiles, few, TILE), bf16),
         pltpu.VMEM((2,) + ids.shape, jnp.int32),
         pltpu.VMEM((dps, 2) + ids.shape, jnp.int32),
         pltpu.SMEM((dps, 2) + ids.shape, jnp.int32),
         dma((4,)), dma, dma((2,)), dma,
         dma((chunks, 2)), dma((chunks, 2)),
-        dma((2, chunks)), dma((2, chunks)),
-        dma((dps, chunks)), dma((dps, chunks)),
-        dma((2, chunks)), dma((3, chunks)),
-        dma((dps, chunks)), dma((dps, chunks)),
+        dma((2, steps)), dma((2, steps)),
+        dma((dps, steps)), dma((dps, steps)),
+        dma((2, steps)), dma((3, steps)),
+        dma((dps, steps)), dma((dps, steps)),
         dma, dma, dma((dps,)), dma((dps,)),
-        dma((tiles,)), dma((tiles,)),
+        dma((2, tiles)), dma((2, tiles)),
     ]
     flops = 2 * rows * feat * width + 2 * 2 * rows * feat * (8 * rows + dps * 6 * RETR)
     result = pl.pallas_call(

time: 49.5 us -> 53.9 us (1.089)
  Pallas kernels: 47.4 us -> 51.7 us
    pallas_call x1, Pallas kernels: 47.4 us -> 51.7 us  [fused_device(): pl.pallas_call(layer_kernel, out_shape=jax.ShapeDtypeStruct((rows, half),...]
where the time goes in v4:
time: 53.9 us; the launch traced here: 53.6 us
  Pallas kernels  51.7 us (96%)
  local copies, waits for them, and re-layouts  1.88 us (3%)
    pallas_call x1, Pallas kernels, fused_device(): pl.pallas_call(layer_kernel, out_shape=jax.ShapeDtypeStruct((rows, half),...  51.7 us
    unnamed x1, local copies, waits for them, and re-layouts  1.88 us

profile of v4, /device:TPU:8, one launch (start us, length us, event | category | flops | bytes accessed | tf_op | source)
XLA Modules:
  0.0 53.6 jit_solution(607043484669634281)
XLA Ops:
  0.0 51.7 %shard_map.73 = bf16[128,2048]{1,0:T(8,128)(2,1)} custom-call(bf16[128,1024]{1,0:T(8,128)(2,1)} %bitcast.9, bf16[128,1024]{1,0:T(8,128)(2,1)} %bitcast.10, bf16[128,1024]{1,0:T(8,128)(2,1)} %bitcast.11, bf16[128,1024]{1,0:T(8,128)(2,1)} %bitcast.12, s32[2,2,2]{2,1,0:T(2,128)} %bitcast.13, bf16[2,6,128,1024]{3,2,1,0:T(8,128)(2,1)} %bitcast.7, ...), custom_call_target="tpu_custom_call" | custom-call | flops 3221225472 | bytes 11534336 | tf_op jit(solution)/shard_map/pallas_call | solution.py:627
  51.7 1.9 %copy.9 = bf16[1,128,2048]{2,1,0:T(8,128)(2,1)} copy(bf16[1,128,2048]{2,1,0:T(8,128)(2,1)} %bitcast.8) | data formatting | bytes 1048576

commit v5 on v3

--- a/solution.py
+++ b/solution.py
@@ -399,11 +399,42 @@
     in_last = lane == 2 * SPAN - 1
     live = jnp.logical_or(lane >= SPAN - 1, s > 0)
 
+    def forward(c):
+        cq_hop(c, 2).wait_recv()
+        cq_hop(c, 3).start()
+
+    def send_merged(c):
+        cp_hop(c, 3).wait_recv()
+        both = [ctx[2, c], cp[3, c]]
+        ctx[2, c] = pack_piece([merge_pieces(both, h) for h in range(2)])
+        cp_hop(c, 2).start()
+
+    def finish(c):
+        @pl.when(s >= 2)
+        def _():
+            sp_hop(c, 0, 2, 1).wait_recv()
+
+        @pl.when(s == 3)
+        def _():
+            sp_hop(c, 0, 3, 2).wait_recv()
+
+        cp_hop(c, 1).wait_recv()
+        cp_hop(c, 2).wait_recv()
+        self_pieces = [sp[i, c] for i in range(3)]
+        cross_pieces = [ctx[0, c], cp[1, c], cp[2, c]]
+        for h in range(2):
+            both = merge_pieces(self_pieces, h)[0] + merge_pieces(cross_pieces, h)[0]
+            att[:, pl.ds(pl.multiple_of(c * PAIR + h * HD, HD), HD)] = both.T.astype(jnp.bfloat16)
+
+    forward(0)
+
     @pl.loop(0, chunks)
     def _(c):
         cols = cols_of(c)
-        cq_hop(c, 2).wait_recv()
-        cq_hop(c, 3).start()
+
+        @pl.when(c + 1 < chunks)
+        def _():
+            forward(c + 1)
 
         @pl.when(s == 1)
         def _():
@@ -446,36 +477,26 @@
             return cross_pair(asked, keys, vts, owned, in_first, in_last, scale)
 
         cq_hop(c, 3).wait_recv()
-        across, beside = cross_part(2), cross_part(3)
-        ctx[3, c] = beside
+        cq_hop(c, 1).wait_recv()
+        parts = [cross_part(j) for j in (3, 2, 1, 0)]
+        for j, part in zip((3, 2, 1, 0), parts):
+            ctx[j, c] = part
         cp_hop(c, 3).start()
-        cq_hop(c, 1).wait_recv()
-        near, own = cross_part(1), cross_part(0)
-        ctx[1, c] = near
-        ctx[0, c] = own
         cp_hop(c, 1).start()
-        cp_hop(c, 3).wait_recv()
-        both = [across, cp[3, c]]
-        ctx[2, c] = pack_piece([merge_pieces(both, h) for h in range(2)])
-        cp_hop(c, 2).start()
-
-    @pl.loop(0, chunks)
+
+        @pl.when(c > 0)
+        def _():
+            send_merged(c - 1)
+
+        @pl.when(c > 1)
+        def _():
+            finish(c - 2)
+
+    send_merged(chunks - 1)
+
+    @pl.loop(chunks - 2, chunks)
     def _(c):
-        @pl.when(s >= 2)
-        def _():
-            sp_hop(c, 0, 2, 1).wait_recv()
-
-        @pl.when(s == 3)
-        def _():
-            sp_hop(c, 0, 3, 2).wait_recv()
-
-        cp_hop(c, 1).wait_recv()
-        cp_hop(c, 2).wait_recv()
-        self_pieces = [sp[i, c] for i in range(3)]
-        cross_pieces = [ctx[0, c], cp[1, c], cp[2, c]]
-        for h in range(2):
-            both = merge_pieces(self_pieces, h)[0] + merge_pieces(cross_pieces, h)[0]
-            att[:, pl.ds(pl.multiple_of(c * PAIR + h * HD, HD), HD)] = both.T.astype(jnp.bfloat16)
+        finish(c)
 
     def tile_cols(t):
         return pl.ds(pl.multiple_of(t * TILE, TILE), TILE)

time: 49.5 us -> 50.3 us (1.016)
  Pallas kernels: 47.4 us -> 48.3 us
    pallas_call x1, Pallas kernels: 47.4 us -> 48.3 us  [fused_device(): pl.pallas_call(layer_kernel, out_shape=jax.ShapeDtypeStruct((rows, half),...]
where the time goes in v5:
time: 50.3 us; the launch traced here: 50.1 us
  Pallas kernels  48.3 us (96%)
  local copies, waits for them, and re-layouts  1.88 us (4%)
    pallas_call x1, Pallas kernels, fused_device(): pl.pallas_call(layer_kernel, out_shape=jax.ShapeDtypeStruct((rows, half),...  48.3 us
    unnamed x1, local copies, waits for them, and re-layouts  1.88 us

profile of v5, /device:TPU:8, one launch (start us, length us, event | category | flops | bytes accessed | tf_op | source)
XLA Modules:
  0.0 50.1 jit_solution(1373577659539974383)
XLA Ops:
  0.0 48.3 %shard_map.73 = bf16[128,2048]{1,0:T(8,128)(2,1)} custom-call(bf16[128,1024]{1,0:T(8,128)(2,1)} %bitcast.9, bf16[128,1024]{1,0:T(8,128)(2,1)} %bitcast.10, bf16[128,1024]{1,0:T(8,128)(2,1)} %bitcast.11, bf16[128,1024]{1,0:T(8,128)(2,1)} %bitcast.12, s32[2,2,2]{2,1,0:T(2,128)} %bitcast.13, bf16[2,6,128,1024]{3,2,1,0:T(8,128)(2,1)} %bitcast.7, ...), custom_call_target="tpu_custom_call" | custom-call | flops 3221225472 | bytes 11534336 | tf_op jit(solution)/shard_map/pallas_call | solution.py:606
  48.3 1.9 %copy.9 = bf16[1,128,2048]{2,1,0:T(8,128)(2,1)} copy(bf16[1,128,2048]{2,1,0:T(8,128)(2,1)} %bitcast.8) | data formatting | bytes 1048576

commit v6 on v3

--- a/solution.py
+++ b/solution.py
@@ -199,23 +199,29 @@
     return pack_piece(parts)
 
 
-def cross_pair(q, keys, vts, owned, in_first, in_last, scale):
-    both = by_head(q)
-    s0, s1, s2 = [nt_dot(k, both) for k in keys]
-    scores = jnp.where(in_first, s0, jnp.where(in_last, s2, s1))
+def cross_pair(q, keys, vts, owned, first, scale):
+    few = q.shape[0] // 2
+    early, late = by_head(q[:few]), by_head(q[few:])
+    late = jnp.concatenate([late[few:], late[:few]], axis=0)
+    scores = jnp.concatenate(
+        [nt_dot(keys[0], early), jnp.where(first, nt_dot(keys[1], late), nt_dot(keys[2], late))], axis=1
+    )
     scores = jnp.where(owned, scores, NEG)
     low, top, total = weigh(scores, scale)
     some = top > 0.5 * NEG
     lse = jnp.where(some, top * scale + jnp.log2(total), NEG)
     inverse = jnp.where(some, 1.0 / total, 0.0)
-    rows = q.shape[0]
-    parts = []
-    for h in range(2):
-        lanes = slice(h * rows, (h + 1) * rows)
-        o0, o1, o2 = [nn_dot(vt[h * HD : (h + 1) * HD], low[:, lanes]) for vt in vts]
-        summed = jnp.where(in_first[:, lanes], o0, jnp.where(in_last[:, lanes], o2, o1))
-        parts.append((summed * inverse[:, lanes], lse[:, lanes]))
-    return pack_piece(parts)
+    lanes = 2 * few
+    early = nn_dot(vts[0], low[:, :lanes]) * inverse[:, :lanes]
+    late = jnp.where(first, nn_dot(vts[1], low[:, lanes:]), nn_dot(vts[2], low[:, lanes:]))
+    late = late * inverse[:, lanes:]
+    left = lax.broadcasted_iota(jnp.int32, (1, lanes), 1) < few
+    return pack_piece(
+        [
+            (jnp.where(left, early[:HD], late[:HD]), jnp.where(left, lse[:, :lanes], lse[:, lanes:])),
+            (jnp.where(left, late[HD:], early[HD:]), jnp.where(left, lse[:, lanes:], lse[:, :lanes])),
+        ]
+    )
 
 
 def merge_pieces(pieces, h):
@@ -235,7 +241,7 @@
 
 def layer_kernel(
     q_hbm, k_hbm, v_hbm, cq_hbm, ids, db_hbm, w_hbm, out,
-    q, k, v, cq, vt, dvt, db, w, k0, vt0, qin, cqin, sp, stx, cp, ctx, att, ptx, prx, ids_tx, ids_rx, ids_s,
+    q, k, v, cq, cqr, vt, dvt, db, w, k0, vt0, qin, cqin, sp, stx, cp, ctx, att, ptx, prx, ids_tx, ids_rx, ids_s,
     in_sem, db_sem, w_sem, ids_sem, kv_ss, kv_rs, q_ss, q_rs, cq_ss, cq_rs, sp_ss, sp_rs, cp_ss, cp_rs,
     i1_ss, i1_rs, i2_ss, i2_rs, p_ss, p_rs,
 ):
@@ -286,10 +292,15 @@
     def turned(block):
         return jnp.concatenate([block[:, :HD].T, block[:, HD:].T], axis=0)
 
+    turn = SPAN - 1
+    few = rows // 2
     in_copies[0].wait()
+    in_copies[1].wait()
 
     @pl.loop(0, chunks)
     def _(c):
+        moved = pltpu.roll(cq[:, cols_of(c)].astype(jnp.float32), rows - turn, axis=0)
+        cqr[c] = moved.astype(jnp.bfloat16)
         vt[c] = turned(v[:, cols_of(c)])
 
     pl.semaphore_wait(barrier, dps + 3)
@@ -309,7 +320,7 @@
         remote(q_hbm.at[:, cols_of(c)], qin.at[slot, c], q_ss.at[0, c], q_rs.at[slot, c], seq=1).wait_recv()
 
     def cq_hop(c, j):
-        src = cqin.at[2, c] if j == 3 else cq_hbm.at[:, cols_of(c)]
+        src = cqin.at[2, c] if j == 3 else cqr.at[c]
         return remote(src, cqin.at[j, c], cq_ss.at[j, c], cq_rs.at[j, c], dp=peer(1 if j == 3 else j))
 
     def sp_hop(c, slot, dest, place):
@@ -371,7 +382,7 @@
     key_at = lax.broadcasted_iota(jnp.int32, (rows, 2 * rows), 0)
     query_at = lax.rem(lax.broadcasted_iota(jnp.int32, (rows, 2 * rows), 1), rows)
     causal = key_at <= query_at
-    for copy in in_copies[1:]:
+    for copy in in_copies[2:]:
         copy.wait()
 
     @pl.loop(0, chunks)
@@ -394,10 +405,7 @@
     ids_copy.wait()
     db_copy.wait()
 
-    lane = lax.rem(lax.broadcasted_iota(jnp.int32, (1, 2 * rows), 1), rows)
-    in_first = lane < SPAN - 1
-    in_last = lane == 2 * SPAN - 1
-    live = jnp.logical_or(lane >= SPAN - 1, s > 0)
+    at_start = lax.rem(lax.broadcasted_iota(jnp.int32, (1, rows), 1), few) == 0
 
     @pl.loop(0, chunks)
     def _(c):
@@ -431,19 +439,21 @@
 
         def cross_part(j):
             keys, vts, shards = [], [], []
-            for which, span in ((1, 1), (0, 0), (0, 1)):
+            for which, span in ((0, 0), (0, 1), (1, 1)):
                 blocks = [ids_s[j, which, span, n, 1] for n in range(NEIGH)]
                 shards.append([ids_s[j, which, span, n, 0] for n in range(NEIGH)])
                 keys.append(jnp.concatenate([db[0, b, :, cols] for b in blocks], axis=0))
                 vts.append(jnp.concatenate([dvt[b] for b in blocks], axis=1))
             owned = []
             for n in range(NEIGH):
-                shard = jnp.where(in_first, shards[0][n], jnp.where(in_last, shards[2][n], shards[1][n]))
-                row = jnp.where(jnp.logical_and(shard == d, live), 1, 0)
+                early = jnp.broadcast_to(shards[0][n], (1, rows)) == d
+                late = jnp.where(at_start, shards[1][n], shards[2][n]) == d
+                late = jnp.logical_and(late, jnp.logical_or(at_start, s > 0))
+                row = jnp.concatenate([jnp.where(early, 1, 0), jnp.where(late, 1, 0)], axis=1)
                 owned.append(jnp.broadcast_to(row, (RETR, 2 * rows)))
             owned = jnp.concatenate(owned, axis=0) > 0
-            asked = cq[:, cols] if j == 0 else cqin[j, c]
-            return cross_pair(asked, keys, vts, owned, in_first, in_last, scale)
+            asked = cqr[c] if j == 0 else cqin[j, c]
+            return cross_pair(asked, keys, vts, owned, at_start, scale)
 
         cq_hop(c, 3).wait_recv()
         across, beside = cross_part(2), cross_part(3)
@@ -474,8 +484,10 @@
         self_pieces = [sp[i, c] for i in range(3)]
         cross_pieces = [ctx[0, c], cp[1, c], cp[2, c]]
         for h in range(2):
-            both = merge_pieces(self_pieces, h)[0] + merge_pieces(cross_pieces, h)[0]
-            att[:, pl.ds(pl.multiple_of(c * PAIR + h * HD, HD), HD)] = both.T.astype(jnp.bfloat16)
+            back = (turn, rows - 1)[h]
+            both = merge_pieces(self_pieces, h)[0].T
+            both = both + pltpu.roll(merge_pieces(cross_pieces, h)[0].T, back, axis=0)
+            att[:, pl.ds(pl.multiple_of(c * PAIR + h * HD, HD), HD)] = both.astype(jnp.bfloat16)
 
     def tile_cols(t):
         return pl.ds(pl.multiple_of(t * TILE, TILE), TILE)
@@ -554,6 +566,7 @@
         pltpu.VMEM((rows, feat), bf16),
         pltpu.VMEM((rows, feat), bf16),
         pltpu.VMEM((rows, feat), bf16),
+        pltpu.VMEM((chunks, rows, PAIR), bf16),
         pltpu.VMEM((chunks, PAIR, rows), bf16),
         pltpu.VMEM((database.shape[2], PAIR, RETR), bf16),
         pltpu.VMEM(database.shape[1:], bf16),

time: 49.5 us -> 48.2 us (0.974)
  Pallas kernels: 47.4 us -> 46.2 us
    pallas_call x1, Pallas kernels: 47.4 us -> 46.2 us  [fused_device(): pl.pallas_call(layer_kernel, out_shape=jax.ShapeDtypeStruct((rows, half),...]
where the time goes in v6:
time: 48.2 us; the launch traced here: 48.1 us
  Pallas kernels  46.2 us (96%)
  local copies, waits for them, and re-layouts  1.88 us (4%)
    pallas_call x1, Pallas kernels, fused_device(): pl.pallas_call(layer_kernel, out_shape=jax.ShapeDtypeStruct((rows, half),...  46.2 us
    unnamed x1, local copies, waits for them, and re-layouts  1.88 us

profile of v6, /device:TPU:8, one launch (start us, length us, event | category | flops | bytes accessed | tf_op | source)
XLA Modules:
  0.0 48.1 jit_solution(188202772980964916)
XLA Ops:
  0.0 46.2 %shard_map.73 = bf16[128,2048]{1,0:T(8,128)(2,1)} custom-call(bf16[128,1024]{1,0:T(8,128)(2,1)} %bitcast.9, bf16[128,1024]{1,0:T(8,128)(2,1)} %bitcast.10, bf16[128,1024]{1,0:T(8,128)(2,1)} %bitcast.11, bf16[128,1024]{1,0:T(8,128)(2,1)} %bitcast.12, s32[2,2,2]{2,1,0:T(2,128)} %bitcast.13, bf16[2,6,128,1024]{3,2,1,0:T(8,128)(2,1)} %bitcast.7, ...), custom_call_target="tpu_custom_call" | custom-call | flops 3221225472 | bytes 11534336 | tf_op jit(solution)/shard_map/pallas_call | solution.py:598
  46.2 1.9 %copy.9 = bf16[1,128,2048]{2,1,0:T(8,128)(2,1)} copy(bf16[1,128,2048]{2,1,0:T(8,128)(2,1)} %bitcast.8) | data formatting | bytes 1048576

commit v7 on v6

--- a/solution.py
+++ b/solution.py
@@ -405,13 +405,22 @@
     ids_copy.wait()
     db_copy.wait()
 
+    def forward(c):
+        cq_hop(c, 2).wait_recv()
+        cq_hop(c, 3).start()
+
+    def send_merged(c):
+        cp_hop(c, 3).wait_recv()
+        both = [ctx[2, c], cp[3, c]]
+        ctx[2, c] = pack_piece([merge_pieces(both, h) for h in range(2)])
+        cp_hop(c, 2).start()
+
+    forward(0)
     at_start = lax.rem(lax.broadcasted_iota(jnp.int32, (1, rows), 1), few) == 0
 
     @pl.loop(0, chunks)
     def _(c):
         cols = cols_of(c)
-        cq_hop(c, 2).wait_recv()
-        cq_hop(c, 3).start()
 
         @pl.when(s == 1)
         def _():
@@ -457,17 +466,25 @@
 
         cq_hop(c, 3).wait_recv()
         across, beside = cross_part(2), cross_part(3)
+        ctx[2, c] = across
         ctx[3, c] = beside
         cp_hop(c, 3).start()
+
+        @pl.when(c + 1 < chunks)
+        def _():
+            forward(c + 1)
+
+        @pl.when(c > 0)
+        def _():
+            send_merged(c - 1)
+
         cq_hop(c, 1).wait_recv()
         near, own = cross_part(1), cross_part(0)
         ctx[1, c] = near
         ctx[0, c] = own
         cp_hop(c, 1).start()
-        cp_hop(c, 3).wait_recv()
-        both = [across, cp[3, c]]
-        ctx[2, c] = pack_piece([merge_pieces(both, h) for h in range(2)])
-        cp_hop(c, 2).start()
+
+    send_merged(chunks - 1)
 
     @pl.loop(0, chunks)
     def _(c):

time: 48.2 us -> 48.4 us (level)
  no operation moved by 1% of the time
where the time goes in v7:
time: 48.4 us; the launch traced here: 48.2 us
  Pallas kernels  46.3 us (96%)
  local copies, waits for them, and re-layouts  1.88 us (4%)
    pallas_call x1, Pallas kernels, fused_device(): pl.pallas_call(layer_kernel, out_shape=jax.ShapeDtypeStruct((rows, half),...  46.3 us
    unnamed x1, local copies, waits for them, and re-layouts  1.88 us

profile of v7, /device:TPU:8, one launch (start us, length us, event | category | flops | bytes accessed | tf_op | source)
XLA Modules:
  0.0 48.2 jit_solution(11694106958392325601)
XLA Ops:
  0.0 46.3 %shard_map.73 = bf16[128,2048]{1,0:T(8,128)(2,1)} custom-call(bf16[128,1024]{1,0:T(8,128)(2,1)} %bitcast.9, bf16[128,1024]{1,0:T(8,128)(2,1)} %bitcast.10, bf16[128,1024]{1,0:T(8,128)(2,1)} %bitcast.11, bf16[128,1024]{1,0:T(8,128)(2,1)} %bitcast.12, s32[2,2,2]{2,1,0:T(2,128)} %bitcast.13, bf16[2,6,128,1024]{3,2,1,0:T(8,128)(2,1)} %bitcast.7, ...), custom_call_target="tpu_custom_call" | custom-call | flops 3221225472 | bytes 11534336 | tf_op jit(solution)/shard_map/pallas_call | solution.py:615
  46.3 1.9 %copy.9 = bf16[1,128,2048]{2,1,0:T(8,128)(2,1)} copy(bf16[1,128,2048]{2,1,0:T(8,128)(2,1)} %bitcast.8) | data formatting | bytes 1048576

commit v8 on v6

--- a/solution.py
+++ b/solution.py
@@ -138,7 +138,7 @@
 LOG2E = 1.4426950408889634
 PAIR = 2 * HD
 PIECE = PAIR + 16
-TILE = 512
+TILE = 256
 MESH = pl.DeviceIdType.MESH
 
 

time: 48.2 us -> 48.2 us (level)
  no operation moved by 1% of the time
where the time goes in v8:
time: 48.2 us; the launch traced here: 48 us
  Pallas kernels  46.1 us (96%)
  local copies, waits for them, and re-layouts  1.88 us (4%)
    pallas_call x1, Pallas kernels, fused_device(): pl.pallas_call(layer_kernel, out_shape=jax.ShapeDtypeStruct((rows, half),...  46.1 us
    unnamed x1, local copies, waits for them, and re-layouts  1.88 us

profile of v8, /device:TPU:8, one launch (start us, length us, event | category | flops | bytes accessed | tf_op | source)
XLA Modules:
  0.0 48.0 jit_solution(3437964364778610239)
XLA Ops:
  0.0 46.1 %shard_map.73 = bf16[128,2048]{1,0:T(8,128)(2,1)} custom-call(bf16[128,1024]{1,0:T(8,128)(2,1)} %bitcast.9, bf16[128,1024]{1,0:T(8,128)(2,1)} %bitcast.10, bf16[128,1024]{1,0:T(8,128)(2,1)} %bitcast.11, bf16[128,1024]{1,0:T(8,128)(2,1)} %bitcast.12, s32[2,2,2]{2,1,0:T(2,128)} %bitcast.13, bf16[2,6,128,1024]{3,2,1,0:T(8,128)(2,1)} %bitcast.7, ...), custom_call_target="tpu_custom_call" | custom-call | flops 3221225472 | bytes 11534336 | tf_op jit(solution)/shard_map/pallas_call | solution.py:598
  46.1 1.9 %copy.9 = bf16[1,128,2048]{2,1,0:T(8,128)(2,1)} copy(bf16[1,128,2048]{2,1,0:T(8,128)(2,1)} %bitcast.8) | data formatting | bytes 1048576
